TPU v7x, 256 devices: a whole 4x4x8 slice. The times are simulated.
256 devices in a mesh: dp: 4 (over y), cache: 8 (over x, core), tensor: 8 (over z).
Axes of the slice: x: 4, y: 4, z: 8, core: 2. Of those that a mesh axis runs over, the one named last changes fastest.
Arguments:
- queries: bfloat16 [32, 256, 16384], P(('dp', 'cache'), None, 'tensor'), may hold values from -6 to 6
- suffix_keys: bfloat16 [32, 256, 1024], P(('dp', 'cache'), None, 'tensor'), may hold values from -12 to 12
- suffix_values: bfloat16 [32, 256, 1024], P(('dp', 'cache'), None, 'tensor'), may hold values from -16 to 16
- prefix_keys: bfloat16 [32, 32, 128, 1024], P(('dp', 'cache'), None, None, 'tensor'), may hold values from -12 to 12
- prefix_values: bfloat16 [32, 32, 128, 1024], P(('dp', 'cache'), None, None, 'tensor'), may hold values from -16 to 16
- hit_len: int32 [32], replicated, may hold values from 1 to 4096, 65536 in all
- suffix_len: int32 [32], replicated, may hold values from 1 to 256, 4096 in all
- page_map: int32 [32, 32], replicated, may hold values from 0 to 31, each once within a row
Outputs:
- attended: bfloat16 [32, 256, 16384], P(('dp', 'cache'), 'tensor')
Inputs may be any that keep to these rules, and one draw needn't show every extreme that they name: Each row of page_map names every holder once: the device of dp+cache with index page_map[r, p] holds page p of request r, at slot r of its prefix arrays.
All inputs are finite; a program needn't handle non-finite values.
Results may differ from a plain program's by a relative error of at most 0.006.
Values may be sent and summed in bfloat16 or wider, within the bound.
No kernel may reach another device: no remote copies, remote signals or barrier semaphores. Data moves between devices by JAX's collectives and lax.ppermute only.
A program may use at most 64 MiB of HBM per device.

v0:
```python
import math

import jax
import jax.numpy as jnp
from jax import lax
from jax.sharding import PartitionSpec as P

HD = 128


def block_update(running, query_lattice, key_tile_rows, value_tile_rows, key_valid, score_scale):
    row_best, row_total, row_accum = running
    scores = (
        jnp.einsum(
            "pojx,mox->opjm", query_lattice, key_tile_rows, preferred_element_type=jnp.float32
        )
        * score_scale
    )
    scores = jnp.where(key_valid, scores, -jnp.inf)
    new_best = jnp.maximum(row_best, jnp.max(scores, axis=-1))
    shrink = jnp.exp(row_best - new_best)
    exp_weights = jnp.exp(scores - new_best[..., None])
    row_total = row_total * shrink + jnp.sum(exp_weights, axis=-1)
    attention_weights = exp_weights.astype(jnp.bfloat16)
    row_accum = row_accum * shrink[..., None] + jnp.einsum(
        "xmar,rxo->xmao", attention_weights, value_tile_rows, preferred_element_type=jnp.float32
    )
    return (new_best, row_total, row_accum)


def local(
    queries, suffix_keys, suffix_values, prefix_keys, prefix_values, hit_len, suffix_len, page_map
):
    requester = lax.axis_index(("dp", "cache"))
    holders = lax.axis_size(("dp", "cache"))
    held_keys = prefix_keys[0]
    held_values = prefix_values[0]
    fetched_keys, fetched_values = (
        lax.all_to_all(held_keys, ("dp", "cache"), split_axis=0, concat_axis=0, tiled=True),
        lax.all_to_all(held_values, ("dp", "cache"), split_axis=0, concat_axis=0, tiled=True),
    )
    page_size = fetched_keys.shape[1]
    kv_width = fetched_keys.shape[2]
    key_heads = kv_width // HD
    suffix = queries.shape[1]
    query_width = queries.shape[2]
    group_size = query_width // kv_width
    key_count = holders * page_size
    score_scale = 1.0 / math.sqrt(HD)
    query_lattice = queries[0].reshape(suffix, key_heads, group_size, HD)
    hit_count = lax.dynamic_index_in_dim(hit_len, requester, 0, keepdims=False)
    live_length = lax.dynamic_index_in_dim(suffix_len, requester, 0, keepdims=False)
    route_row = lax.dynamic_index_in_dim(page_map, requester, 0, keepdims=False)
    slot_ids = jnp.arange(page_size, dtype=jnp.int32)
    positions = jnp.arange(suffix, dtype=jnp.int32)
    causal_mask = positions[None, :] <= positions[:, None]
    running = (
        jnp.full((key_heads, suffix, group_size), -1e30, jnp.float32),
        jnp.zeros((key_heads, suffix, group_size), jnp.float32),
        jnp.zeros((key_heads, suffix, group_size, HD), jnp.float32),
    )
    running = block_update(
        running,
        query_lattice,
        suffix_keys[0].reshape(suffix, key_heads, HD),
        suffix_values[0].reshape(suffix, key_heads, HD),
        causal_mask[None, :, None, :],
        score_scale,
    )
    keys_in_block = 512
    holder_ids = jnp.arange(holders, dtype=jnp.int32)
    holder_match = (route_row[None, :] == holder_ids[:, None]).astype(jnp.int32)
    page_index = jnp.sum(holder_match * holder_ids[None, :], axis=1)
    ordered_keys = fetched_keys.reshape(key_count, key_heads, HD)
    ordered_values = fetched_values.reshape(key_count, key_heads, HD)
    key_position = (page_index[:, None] * page_size + slot_ids[None, :]).reshape(key_count)
    block_count = key_count // keys_in_block

    def visit(block_number, running):
        block_offset = block_number * keys_in_block
        key_tile_rows = lax.dynamic_slice_in_dim(ordered_keys, block_offset, keys_in_block, 0)
        value_tile_rows = lax.dynamic_slice_in_dim(ordered_values, block_offset, keys_in_block, 0)
        key_valid = (
            lax.dynamic_slice_in_dim(key_position, block_offset, keys_in_block, 0) < hit_count
        )
        return block_update(
            running,
            query_lattice,
            key_tile_rows,
            value_tile_rows,
            key_valid[None, None, None, :],
            score_scale,
        )

    row_best, row_total, row_accum = lax.fori_loop(0, block_count, visit, running)
    result = row_accum / row_total[..., None]
    live_rows = positions < live_length
    result = jnp.where(live_rows[None, :, None, None], result, jnp.zeros_like(result))
    result = (
        jnp.transpose(result, (1, 0, 2, 3)).reshape(1, suffix, query_width).astype(jnp.bfloat16)
    )
    return lax.all_to_all(result, "tensor", split_axis=1, concat_axis=2, tiled=True)


def solution(mesh):
    placed = (
        P(("dp", "cache"), None, "tensor"),
        P(("dp", "cache"), None, "tensor"),
        P(("dp", "cache"), None, "tensor"),
        P(("dp", "cache"), None, None, "tensor"),
        P(("dp", "cache"), None, None, "tensor"),
        P(),
        P(),
        P(),
    )
    return jax.shard_map(
        local,
        mesh=mesh,
        in_specs=placed,
        out_specs=P(("dp", "cache"), "tensor", None),
        check_vma=False,
    )
```

profile of v0, /device:TPU:1, one launch (start us, length us, event | category | flops | bytes accessed | tf_op | source)
XLA Modules:
  0.0 168.5 jit_solution(2277822267035764132)
XLA Ops:
  0.0 8.7 %all-to-all-start = ((bf16[32,128,128]{2,1,0:T(8,128)(2,1)}), bf16[32,128,128]{2,1,0:T(8,128)(2,1)S(1)}, u32[]{:S(2)}, u32[]{:S(2)}) async-start(bf16[32,128,128]{2,1,0:T(8,128)(2,1)} %bitcast.107), calls=%async_computation | async-start | bytes 2097152 | tf_op jit(solution)/shard_map/all_to_all | solution.py:39
  8.8 1.5 copy.47
  10.3 0.8 dynamic-slice_bitcast_fusion
  11.2 0.6 dynamic_slice.32
  11.8 2.7 %fusion.19 = (f32[256,16]{0,1:T(8,128)S(1)}, f32[256,16,256]{0,2,1:T(8,128)}) fusion(pred[256,256]{0,1:T(8,128)(4,1)S(1)} %iota_compare_fusion, bf16[1,256,128]{2,1,0:T(8,128)(2,1)S(1)} %copy-done, bf16[256,16,128]{2,1,0:T(8,128)(2,1)S(1)} %bitcast.105), kind=kOutput, calls=%fused_computation.26 | convolution fusion | flops 271577088 | bytes 5390336 | tf_op jit(solution)/shard_map/pojx,mox->opjm/dot_general | solution.py:14
  14.6 11.3 %all-to-all-done = bf16[32,128,128]{2,1,0:T(8,128)(2,1)S(1)} async-done(((bf16[32,128,128]{2,1,0:T(8,128)(2,1)}), bf16[32,128,128]{2,1,0:T(8,128)(2,1)S(1)}, u32[]{:S(2)}, u32[]{:S(2)}) %all-to-all-start) | async-done | bytes 1048608 | tf_op jit(solution)/shard_map/all_to_all | solution.py:39
  25.9 4.6 %all-to-all-start.1 = ((bf16[32,128,128]{2,1,0:T(8,128)(2,1)}), bf16[32,128,128]{2,1,0:T(8,128)(2,1)}, u32[]{:S(2)}, u32[]{:S(2)}) async-start(bf16[32,128,128]{2,1,0:T(8,128)(2,1)} %bitcast.108), calls=%async_computation.1 | async-start | bytes 2097152 | tf_op jit(solution)/shard_map/all_to_all | solution.py:40
  30.6 0.7 iota_compare_fusion.2
  31.2 0.5 copy.38
  31.8 0.6 dynamic_slice.34
  32.4 0.7 copy.39
  33.1 3.2 %fusion.21 = f32[256,16]{0,1:T(8,128)S(1)} fusion(f32[256,16,256]{0,2,1:T(8,128)} %get-tuple-element.224, f32[256,16]{0,1:T(8,128)S(1)} %get-tuple-element.222, pred[256,256]{0,1:T(8,128)(4,1)S(1)} %iota_compare_fusion), kind=kLoop, calls=%fused_computation.28 | loop fusion | flops 4190208 | bytes 4292608 | tf_op jit(solution)/shard_map/reduce_sum | solution.py:23
  36.5 2.6 %add_bitcast_fusion = f32[1,256,16,128]{3,1,2,0:T(8,128)} fusion(f32[256,16,256]{0,2,1:T(8,128)S(1)} %copy-done.1, f32[256,16]{0,1:T(8,128)S(1)} %get-tuple-element.222, pred[256,256]{0,1:T(8,128)(4,1)S(1)} %iota_compare_fusion, f32[256,16]{0,1:T(8,128)S(1)} %get-tuple-element.220, bf16[1,256,128]{2,1,0:T(8,128)(2,1)S(1)} %copy-done.5), kind=kOutput, calls=%fused_computation.31 | convolution fusion | flops 273154048 | bytes 6455296 | tf_op jit(solution)/shard_map/xmar,rxo->xmao/dot_general | solution.py:25
  39.1 8.8 %all-to-all-done.1 = bf16[32,128,128]{2,1,0:T(8,128)(2,1)} async-done(((bf16[32,128,128]{2,1,0:T(8,128)(2,1)}), bf16[32,128,128]{2,1,0:T(8,128)(2,1)}, u32[]{:S(2)}, u32[]{:S(2)}) %all-to-all-start.1) | async-done | bytes 1048608 | tf_op jit(solution)/shard_map/all_to_all | solution.py:40
  47.9 69.6 %while.17 = (s32[]{:T(128)}, f32[1,256,16]{1,2,0:T(8,128)S(1)}, f32[1,256,16]{1,2,0:T(8,128)S(1)}, f32[1,256,16,128]{3,1,2,0:T(8,128)}, s32[4096]{0:T(1024)S(1)}...) while((s32[]{:T(128)}, f32[1,256,16]{1,2,0:T(8,128)S(1)}, ...), condition=%wide.region_6.7_spmd, body=%wide.region_3.6_spmd.sunk | while | flops 1097871872 | bytes 47714548 | solution.py:95
  47.9 0.7 dynamic-slice_compare_fusion.2
  48.6 1.3 bitcast_reduce_fusion.2
  49.9 0.3 copy-done.3
  50.2 4.4 %bitcast_add_fusion.6 = f32[1,256,16,128]{3,1,2,0:T(8,128)S(1)} fusion(f32[1,256,16,128]{3,1,2,0:T(8,128)S(1)} %copy-done.3, f32[512,256,16]{1,0,2:T(8,128)S(1)} %get-tuple-element.286, f32[256,16]{0,1:T(8,128)S(1)} %bitcast.99, pred[512]{0:T(512)(128)(4,1)S(1)} %dynamic-slice_compare_fusion.2, f32[256,16]{0,1:T(8,128)S(1)} %get-tuple-element.287, ...), kind=kOutput, calls=%fused_computation.8.clone.1 | convolution fusion | flops 546308096 | bytes 12747268 | tf_op jit(solution)/shard_map/while/body/eval_jaxpr/xmar,rxo->xmao/dot_general | solution.py:25
  54.6 2.0 %fusion.44 = f32[256,16]{0,1:T(8,128)S(1)} fusion(f32[512,256,16]{1,0,2:T(8,128)S(1)} %get-tuple-element.286, f32[256,16]{0,1:T(8,128)S(1)} %bitcast.100, pred[512]{0:T(512)(128)(4,1)S(1)} %dynamic-slice_compare_fusion.2), kind=kLoop, calls=%fused_computation.5.clone.1 | loop fusion | flops 8384512 | bytes 8421888 | tf_op jit(solution)/shard_map/while/body/eval_jaxpr/reduce_sum | solution.py:23
  56.6 0.7 dynamic-slice_compare_fusion.2
  57.3 1.3 bitcast_reduce_fusion.2
  58.6 0.3 copy-done.3
  58.9 4.4 %bitcast_add_fusion.6 = f32[1,256,16,128]{3,1,2,0:T(8,128)S(1)} fusion(f32[1,256,16,128]{3,1,2,0:T(8,128)S(1)} %copy-done.3, f32[512,256,16]{1,0,2:T(8,128)S(1)} %get-tuple-element.286, f32[256,16]{0,1:T(8,128)S(1)} %bitcast.99, pred[512]{0:T(512)(128)(4,1)S(1)} %dynamic-slice_compare_fusion.2, f32[256,16]{0,1:T(8,128)S(1)} %get-tuple-element.287, ...), kind=kOutput, calls=%fused_computation.8.clone.1 | convolution fusion | flops 546308096 | bytes 12747268 | tf_op jit(solution)/shard_map/while/body/eval_jaxpr/xmar,rxo->xmao/dot_general | solution.py:25
  63.3 2.0 %fusion.44 = f32[256,16]{0,1:T(8,128)S(1)} fusion(f32[512,256,16]{1,0,2:T(8,128)S(1)} %get-tuple-element.286, f32[256,16]{0,1:T(8,128)S(1)} %bitcast.100, pred[512]{0:T(512)(128)(4,1)S(1)} %dynamic-slice_compare_fusion.2), kind=kLoop, calls=%fused_computation.5.clone.1 | loop fusion | flops 8384512 | bytes 8421888 | tf_op jit(solution)/shard_map/while/body/eval_jaxpr/reduce_sum | solution.py:23
  65.3 0.7 dynamic-slice_compare_fusion.2
  66.0 1.3 bitcast_reduce_fusion.2
  67.3 0.3 copy-done.3
  67.6 4.4 %bitcast_add_fusion.6 = f32[1,256,16,128]{3,1,2,0:T(8,128)S(1)} fusion(f32[1,256,16,128]{3,1,2,0:T(8,128)S(1)} %copy-done.3, f32[512,256,16]{1,0,2:T(8,128)S(1)} %get-tuple-element.286, f32[256,16]{0,1:T(8,128)S(1)} %bitcast.99, pred[512]{0:T(512)(128)(4,1)S(1)} %dynamic-slice_compare_fusion.2, f32[256,16]{0,1:T(8,128)S(1)} %get-tuple-element.287, ...), kind=kOutput, calls=%fused_computation.8.clone.1 | convolution fusion | flops 546308096 | bytes 12747268 | tf_op jit(solution)/shard_map/while/body/eval_jaxpr/xmar,rxo->xmao/dot_general | solution.py:25
  72.0 2.0 %fusion.44 = f32[256,16]{0,1:T(8,128)S(1)} fusion(f32[512,256,16]{1,0,2:T(8,128)S(1)} %get-tuple-element.286, f32[256,16]{0,1:T(8,128)S(1)} %bitcast.100, pred[512]{0:T(512)(128)(4,1)S(1)} %dynamic-slice_compare_fusion.2), kind=kLoop, calls=%fused_computation.5.clone.1 | loop fusion | flops 8384512 | bytes 8421888 | tf_op jit(solution)/shard_map/while/body/eval_jaxpr/reduce_sum | solution.py:23
  74.0 0.7 dynamic-slice_compare_fusion.2
  74.7 1.3 bitcast_reduce_fusion.2
  76.0 0.3 copy-done.3
  76.3 4.4 %bitcast_add_fusion.6 = f32[1,256,16,128]{3,1,2,0:T(8,128)S(1)} fusion(f32[1,256,16,128]{3,1,2,0:T(8,128)S(1)} %copy-done.3, f32[512,256,16]{1,0,2:T(8,128)S(1)} %get-tuple-element.286, f32[256,16]{0,1:T(8,128)S(1)} %bitcast.99, pred[512]{0:T(512)(128)(4,1)S(1)} %dynamic-slice_compare_fusion.2, f32[256,16]{0,1:T(8,128)S(1)} %get-tuple-element.287, ...), kind=kOutput, calls=%fused_computation.8.clone.1 | convolution fusion | flops 546308096 | bytes 12747268 | tf_op jit(solution)/shard_map/while/body/eval_jaxpr/xmar,rxo->xmao/dot_general | solution.py:25
  80.7 2.0 %fusion.44 = f32[256,16]{0,1:T(8,128)S(1)} fusion(f32[512,256,16]{1,0,2:T(8,128)S(1)} %get-tuple-element.286, f32[256,16]{0,1:T(8,128)S(1)} %bitcast.100, pred[512]{0:T(512)(128)(4,1)S(1)} %dynamic-slice_compare_fusion.2), kind=kLoop, calls=%fused_computation.5.clone.1 | loop fusion | flops 8384512 | bytes 8421888 | tf_op jit(solution)/shard_map/while/body/eval_jaxpr/reduce_sum | solution.py:23
  82.7 0.7 dynamic-slice_compare_fusion.2
  83.4 1.3 bitcast_reduce_fusion.2
  84.7 0.3 copy-done.3
  85.0 4.4 %bitcast_add_fusion.6 = f32[1,256,16,128]{3,1,2,0:T(8,128)S(1)} fusion(f32[1,256,16,128]{3,1,2,0:T(8,128)S(1)} %copy-done.3, f32[512,256,16]{1,0,2:T(8,128)S(1)} %get-tuple-element.286, f32[256,16]{0,1:T(8,128)S(1)} %bitcast.99, pred[512]{0:T(512)(128)(4,1)S(1)} %dynamic-slice_compare_fusion.2, f32[256,16]{0,1:T(8,128)S(1)} %get-tuple-element.287, ...), kind=kOutput, calls=%fused_computation.8.clone.1 | convolution fusion | flops 546308096 | bytes 12747268 | tf_op jit(solution)/shard_map/while/body/eval_jaxpr/xmar,rxo->xmao/dot_general | solution.py:25
  89.4 2.0 %fusion.44 = f32[256,16]{0,1:T(8,128)S(1)} fusion(f32[512,256,16]{1,0,2:T(8,128)S(1)} %get-tuple-element.286, f32[256,16]{0,1:T(8,128)S(1)} %bitcast.100, pred[512]{0:T(512)(128)(4,1)S(1)} %dynamic-slice_compare_fusion.2), kind=kLoop, calls=%fused_computation.5.clone.1 | loop fusion | flops 8384512 | bytes 8421888 | tf_op jit(solution)/shard_map/while/body/eval_jaxpr/reduce_sum | solution.py:23
  91.4 0.7 dynamic-slice_compare_fusion.2
  92.1 1.3 bitcast_reduce_fusion.2
  93.4 0.3 copy-done.3
  93.7 4.4 %bitcast_add_fusion.6 = f32[1,256,16,128]{3,1,2,0:T(8,128)S(1)} fusion(f32[1,256,16,128]{3,1,2,0:T(8,128)S(1)} %copy-done.3, f32[512,256,16]{1,0,2:T(8,128)S(1)} %get-tuple-element.286, f32[256,16]{0,1:T(8,128)S(1)} %bitcast.99, pred[512]{0:T(512)(128)(4,1)S(1)} %dynamic-slice_compare_fusion.2, f32[256,16]{0,1:T(8,128)S(1)} %get-tuple-element.287, ...), kind=kOutput, calls=%fused_computation.8.clone.1 | convolution fusion | flops 546308096 | bytes 12747268 | tf_op jit(solution)/shard_map/while/body/eval_jaxpr/xmar,rxo->xmao/dot_general | solution.py:25
  98.1 2.0 %fusion.44 = f32[256,16]{0,1:T(8,128)S(1)} fusion(f32[512,256,16]{1,0,2:T(8,128)S(1)} %get-tuple-element.286, f32[256,16]{0,1:T(8,128)S(1)} %bitcast.100, pred[512]{0:T(512)(128)(4,1)S(1)} %dynamic-slice_compare_fusion.2), kind=kLoop, calls=%fused_computation.5.clone.1 | loop fusion | flops 8384512 | bytes 8421888 | tf_op jit(solution)/shard_map/while/body/eval_jaxpr/reduce_sum | solution.py:23
  100.1 0.7 dynamic-slice_compare_fusion.2
  100.8 1.3 bitcast_reduce_fusion.2
  102.1 0.3 copy-done.3
  102.4 4.4 %bitcast_add_fusion.6 = f32[1,256,16,128]{3,1,2,0:T(8,128)S(1)} fusion(f32[1,256,16,128]{3,1,2,0:T(8,128)S(1)} %copy-done.3, f32[512,256,16]{1,0,2:T(8,128)S(1)} %get-tuple-element.286, f32[256,16]{0,1:T(8,128)S(1)} %bitcast.99, pred[512]{0:T(512)(128)(4,1)S(1)} %dynamic-slice_compare_fusion.2, f32[256,16]{0,1:T(8,128)S(1)} %get-tuple-element.287, ...), kind=kOutput, calls=%fused_computation.8.clone.1 | convolution fusion | flops 546308096 | bytes 12747268 | tf_op jit(solution)/shard_map/while/body/eval_jaxpr/xmar,rxo->xmao/dot_general | solution.py:25
  106.8 2.0 %fusion.44 = f32[256,16]{0,1:T(8,128)S(1)} fusion(f32[512,256,16]{1,0,2:T(8,128)S(1)} %get-tuple-element.286, f32[256,16]{0,1:T(8,128)S(1)} %bitcast.100, pred[512]{0:T(512)(128)(4,1)S(1)} %dynamic-slice_compare_fusion.2), kind=kLoop, calls=%fused_computation.5.clone.1 | loop fusion | flops 8384512 | bytes 8421888 | tf_op jit(solution)/shard_map/while/body/eval_jaxpr/reduce_sum | solution.py:23
  108.8 0.7 dynamic-slice_compare_fusion.2
  109.6 1.3 bitcast_reduce_fusion.2
  110.8 0.3 copy-done.3
  111.1 4.4 %bitcast_add_fusion.6 = f32[1,256,16,128]{3,1,2,0:T(8,128)S(1)} fusion(f32[1,256,16,128]{3,1,2,0:T(8,128)S(1)} %copy-done.3, f32[512,256,16]{1,0,2:T(8,128)S(1)} %get-tuple-element.286, f32[256,16]{0,1:T(8,128)S(1)} %bitcast.99, pred[512]{0:T(512)(128)(4,1)S(1)} %dynamic-slice_compare_fusion.2, f32[256,16]{0,1:T(8,128)S(1)} %get-tuple-element.287, ...), kind=kOutput, calls=%fused_computation.8.clone.1 | convolution fusion | flops 546308096 | bytes 12747268 | tf_op jit(solution)/shard_map/while/body/eval_jaxpr/xmar,rxo->xmao/dot_general | solution.py:25
  115.5 2.0 %fusion.44 = f32[256,16]{0,1:T(8,128)S(1)} fusion(f32[512,256,16]{1,0,2:T(8,128)S(1)} %get-tuple-element.286, f32[256,16]{0,1:T(8,128)S(1)} %bitcast.100, pred[512]{0:T(512)(128)(4,1)S(1)} %dynamic-slice_compare_fusion.2), kind=kLoop, calls=%fused_computation.5.clone.1 | loop fusion | flops 8384512 | bytes 8421888 | tf_op jit(solution)/shard_map/while/body/eval_jaxpr/reduce_sum | solution.py:23
  117.5 1.9 %copy.40 = f32[1,256,16,128]{1,3,2,0:T(8,128)S(1)} copy(f32[1,256,16,128]{3,1,2,0:T(8,128)} %get-tuple-element.160) | data formatting | bytes 4194304 | tf_op jit(solution)/shard_map/while | solution.py:95
  119.7 2.2 %copy.41 = bf16[1,256,2048]{2,0,1:T(2,128)(2,1)S(1)} copy(bf16[1,256,2048]{1,2,0:T(8,128)(2,1)S(1)} %bitcast.101) | data formatting | bytes 2097152 | tf_op jit(solution)/shard_map/convert_element_type | solution.py:100
  121.9 0.5 broadcast.119
  122.4 6.8 %reduce.12 = bf16[256,2048]{1,0:T(8,128)(2,1)S(1)} reduce(bf16[256,1,2048]{2,1,0:T(2,128)(2,1)S(1)} %bitcast.98, bf16[]{:T(256)} %broadcast.119), dimensions={1}, to_apply=%bitcast.68.reduce_sub_computation | reduce | bytes 2097154
  129.2 0.8 reshape.177
  130.0 35.8 %all_to_all.28 = bf16[8,2,32768]{2,1,0:T(2,128)(2,1)S(1)} all-to-all(bf16[8,2,32768]{2,1,0:T(2,128)(2,1)S(1)} %reshape.177), channel_id=1, replica_groups=mesh['dp'=4,'cache'=8,'tensor'=8] {'tensor'}, dimensions={0} | all-to-all | bytes 2097152 | tf_op jit(solution)/shard_map/all_to_all | solution.py:102
  165.8 1.0 reshape.178
  166.8 0.6 copy.45
  167.4 1.0 copy.46
  (67 shorter events, 1.0 us)
Async XLA Ops:
  0.0 11.8 %copy-start = (bf16[1,256,128]{2,1,0:T(8,128)(2,1)S(1)}, bf16[1,256,128]{2,1,0:T(8,128)(2,1)}, u32[]{:S(2)}) copy-start(bf16[1,256,128]{2,1,0:T(8,128)(2,1)} %param.11) | copy-start | bytes 196612
  0.0 11.1 %copy-start.6 = (s32[32]{0:T(128)S(1)}, s32[32]{0:T(128)}, u32[]{:S(2)}) copy-start(s32[32]{0:T(128)} %param.16) | copy-start | bytes 388
  0.0 25.9 %all-to-all-start = ((bf16[32,128,128]{2,1,0:T(8,128)(2,1)}), bf16[32,128,128]{2,1,0:T(8,128)(2,1)S(1)}, u32[]{:S(2)}, u32[]{:S(2)}) async-start(bf16[32,128,128]{2,1,0:T(8,128)(2,1)} %bitcast.107), calls=%async_computation | async-start | bytes 2097152 | tf_op jit(solution)/shard_map/all_to_all | solution.py:39
  10.2 21.0 %copy-start.2 = (bf16[1,256,2048]{2,1,0:T(8,128)(2,1)S(1)}, bf16[1,256,2048]{2,1,0:T(8,128)(2,1)}, u32[]{:S(2)}) copy-start(bf16[1,256,2048]{2,1,0:T(8,128)(2,1)} %param.10) | copy-start | bytes 3145732
  11.8 19.9 %copy-start.7 = (s32[32]{0:T(128)S(1)}, s32[32]{0:T(128)}, u32[]{:S(2)}) copy-start(s32[32]{0:T(128)} %param.15) | copy-start | bytes 388
  25.9 22.0 %all-to-all-start.1 = ((bf16[32,128,128]{2,1,0:T(8,128)(2,1)}), bf16[32,128,128]{2,1,0:T(8,128)(2,1)}, u32[]{:S(2)}, u32[]{:S(2)}) async-start(bf16[32,128,128]{2,1,0:T(8,128)(2,1)} %bitcast.108), calls=%async_computation.1 | async-start | bytes 2097152 | tf_op jit(solution)/shard_map/all_to_all | solution.py:40
  31.2 5.1 %copy-start.5 = (bf16[1,256,128]{2,1,0:T(8,128)(2,1)S(1)}, bf16[1,256,128]{2,1,0:T(8,128)(2,1)}, u32[]{:S(2)}) copy-start(bf16[1,256,128]{2,1,0:T(8,128)(2,1)} %param.12) | copy-start | bytes 196612
  33.1 3.5 %copy-start.1 = (f32[256,16,256]{0,2,1:T(8,128)S(1)}, f32[256,16,256]{0,2,1:T(8,128)}, u32[]{:S(2)}) copy-start(f32[256,16,256]{0,2,1:T(8,128)} %get-tuple-element.224) | copy-start | bytes 12582916
  48.6 1.6 copy-start.3
  54.6 2.0 %copy-start.4 = (f32[1,256,16,128]{3,1,2,0:T(8,128)}, f32[1,256,16,128]{3,1,2,0:T(8,128)S(1)}, u32[]{:S(2)}) copy-start(f32[1,256,16,128]{3,1,2,0:T(8,128)S(1)} %bitcast_add_fusion.6) | copy-start | bytes 6291460 | tf_op jit(solution)/shard_map/while
  57.3 1.6 copy-start.3
  63.3 2.0 %copy-start.4 = (f32[1,256,16,128]{3,1,2,0:T(8,128)}, f32[1,256,16,128]{3,1,2,0:T(8,128)S(1)}, u32[]{:S(2)}) copy-start(f32[1,256,16,128]{3,1,2,0:T(8,128)S(1)} %bitcast_add_fusion.6) | copy-start | bytes 6291460 | tf_op jit(solution)/shard_map/while
  66.0 1.6 copy-start.3
  72.0 2.0 %copy-start.4 = (f32[1,256,16,128]{3,1,2,0:T(8,128)}, f32[1,256,16,128]{3,1,2,0:T(8,128)S(1)}, u32[]{:S(2)}) copy-start(f32[1,256,16,128]{3,1,2,0:T(8,128)S(1)} %bitcast_add_fusion.6) | copy-start | bytes 6291460 | tf_op jit(solution)/shard_map/while
  74.7 1.6 copy-start.3
  80.7 2.0 %copy-start.4 = (f32[1,256,16,128]{3,1,2,0:T(8,128)}, f32[1,256,16,128]{3,1,2,0:T(8,128)S(1)}, u32[]{:S(2)}) copy-start(f32[1,256,16,128]{3,1,2,0:T(8,128)S(1)} %bitcast_add_fusion.6) | copy-start | bytes 6291460 | tf_op jit(solution)/shard_map/while
  83.4 1.6 copy-start.3
  89.4 2.0 %copy-start.4 = (f32[1,256,16,128]{3,1,2,0:T(8,128)}, f32[1,256,16,128]{3,1,2,0:T(8,128)S(1)}, u32[]{:S(2)}) copy-start(f32[1,256,16,128]{3,1,2,0:T(8,128)S(1)} %bitcast_add_fusion.6) | copy-start | bytes 6291460 | tf_op jit(solution)/shard_map/while
  92.1 1.6 copy-start.3
  98.1 2.0 %copy-start.4 = (f32[1,256,16,128]{3,1,2,0:T(8,128)}, f32[1,256,16,128]{3,1,2,0:T(8,128)S(1)}, u32[]{:S(2)}) copy-start(f32[1,256,16,128]{3,1,2,0:T(8,128)S(1)} %bitcast_add_fusion.6) | copy-start | bytes 6291460 | tf_op jit(solution)/shard_map/while
  100.8 1.6 copy-start.3
  106.8 2.0 %copy-start.4 = (f32[1,256,16,128]{3,1,2,0:T(8,128)}, f32[1,256,16,128]{3,1,2,0:T(8,128)S(1)}, u32[]{:S(2)}) copy-start(f32[1,256,16,128]{3,1,2,0:T(8,128)S(1)} %bitcast_add_fusion.6) | copy-start | bytes 6291460 | tf_op jit(solution)/shard_map/while
  109.6 1.6 copy-start.3
  115.5 2.0 %copy-start.4 = (f32[1,256,16,128]{3,1,2,0:T(8,128)}, f32[1,256,16,128]{3,1,2,0:T(8,128)S(1)}, u32[]{:S(2)}) copy-start(f32[1,256,16,128]{3,1,2,0:T(8,128)S(1)} %bitcast_add_fusion.6) | copy-start | bytes 6291460 | tf_op jit(solution)/shard_map/while
where the time goes:
time: 169 us; the launch traced here: 168 us
  matrix products  50.2 us (30%)
  blocking collectives  35.8 us (21%)
  other arithmetic  32.7 us (19%)
  waiting for transfers between devices  20.2 us (12%)
  local copies, waits for them, and re-layouts  15.4 us (9%)
  starting transfers between devices  13.4 us (8%)
    dot_general x9, matrix products, block_update(): jnp.einsum('xmar,rxo->xmao', attention_weights, value_tile_rows, preferre...  37.4 us
    all_to_all x1, blocking collectives, local(): lax.all_to_all(result, 'tensor', split_axis=1, concat_axis=2, tiled=True)  35.8 us
    reduce_sum x9, other arithmetic, block_update(): row_total = row_total * shrink + jnp.sum(exp_weights, axis=-1)  18.9 us
    dot_general x9, matrix products, block_update(): jnp.einsum('pojx,mox->opjm', query_lattice, key_tile_rows, preferred_elem...  12.9 us
    all_to_all x1, waiting for transfers between devices, local(): lax.all_to_all(held_keys, ('dp', 'cache'), split_axis=0, concat_axis=0, t...  11.3 us
    all_to_all x1, waiting for transfers between devices, local(): lax.all_to_all(held_values, ('dp', 'cache'), split_axis=0, concat_axis=0,...  8.83 us
    all_to_all x1, starting transfers between devices, local(): lax.all_to_all(held_keys, ('dp', 'cache'), split_axis=0, concat_axis=0, t...  8.72 us
    unnamed x1, other arithmetic  6.79 us
  transfers between devices with their start and end apart: 2, of which 2 were waited for; matrix products, arithmetic and copies ran while one was open for 8% of the time, Pallas kernels for 0%

commit v1 on v0

v1 whole, which is shorter than its diff:
```python
import functools
import math

import jax
import jax.numpy as jnp
from jax import lax
from jax.experimental import pallas as pl
from jax.experimental.pallas import tpu as pltpu
from jax.sharding import PartitionSpec as P

HD = 128
HEADS = 16
WIDTH = HEADS * HD
PAGE = 128
PAGES = 32
KEYS = PAGES * PAGE
SUF = 256
ROWS = 32
RB = ROWS * HEADS
TILE = 1024
RS = 512
GROUPS = ((4, 3, 5), (2, 6, 1, 7), (0,))
SCALE = math.log2(math.e) / math.sqrt(HD)
F32 = jnp.float32
BF16 = jnp.bfloat16
DEVICES = ("dp", "cache")
PARAMS = pltpu.CompilerParams(vmem_limit_bytes=24 << 20)
SMEM = pl.BlockSpec(memory_space=pltpu.SMEM)
VMEM = pl.BlockSpec(memory_space=pltpu.VMEM)


def qk(a, b):
    return lax.dot_general(a, b, (((1,), (1,)), ((), ())), preferred_element_type=F32)


def pv(a, b):
    return lax.dot_general(a, b, (((1,), (0,)), ((), ())), preferred_element_type=F32)


def prepare(place, page_map, buf_ref, sk_ref, k_out, v_out):
    first_key = sk_ref[0:1, :].astype(F32)
    slot = lax.broadcasted_iota(jnp.int32, (PAGE, HD), 0)
    request, hit = place[0], place[2]

    def page(p, _):
        holder = page_map[request, p]
        valid = slot < hit - p * PAGE
        rows = pl.ds(pl.multiple_of(p * PAGE, PAGE), PAGE)
        k_out[rows, :] = jnp.where(valid, buf_ref[holder, :PAGE, :].astype(F32), first_key).astype(BF16)
        v_out[rows, :HD] = jnp.where(valid, buf_ref[holder, PAGE:, :].astype(F32), 0.0).astype(BF16)
        v_out[rows, HD:] = jnp.where(valid, 1.0, 0.0).astype(BF16)
        return 0

    lax.fori_loop(0, PAGES, page, 0, unroll=4)


def row_block(q_ref, t):
    q = jnp.concatenate([q_ref[t, :, n * HD:(n + 1) * HD] for n in range(HEADS)], axis=0)
    scaled = q.astype(F32) * SCALE
    high = scaled.astype(BF16)
    low = (scaled - high.astype(F32)).astype(BF16)
    return jnp.concatenate([high, low], axis=1)


def attend(t, live, q_ref, sk_ref, sv_ref, k_ref, v_ref, o_ref):
    q = row_block(q_ref, t)
    slot = t * ROWS + lax.broadcasted_iota(jnp.int32, (RS, SUF), 0) % ROWS
    causal = lax.broadcasted_iota(jnp.int32, (RS, SUF), 1) <= slot
    parts = RB // RS
    units = [(r, j) for j in range(-1, KEYS // TILE) for r in range(parts)]

    def keys(j):
        return sk_ref[...] if j < 0 else k_ref[j * TILE:(j + 1) * TILE, :]

    def values(j):
        if j < 0:
            return jnp.concatenate([sv_ref[...], jnp.ones((SUF, HD), BF16)], axis=1)
        return v_ref[j * TILE:(j + 1) * TILE, :]

    def score(unit):
        r, j = unit
        s = qk(q[r * RS:(r + 1) * RS], jnp.concatenate([keys(j)] * 2, axis=1))
        return jnp.where(causal, s, -jnp.inf) if j < 0 else s

    best, accum = [None] * parts, [None] * parts
    ahead = score(units[0])
    for i, (r, j) in enumerate(units):
        s = ahead
        if i + 1 < len(units):
            ahead = score(units[i + 1])
        top = jnp.max(s, axis=1, keepdims=True)
        if j < 0:
            best[r] = top
            accum[r] = pv(jnp.exp2(s - top).astype(BF16), values(j))
        else:
            new = jnp.maximum(best[r], top)
            p = jnp.exp2(s - new).astype(BF16)
            accum[r] = accum[r] * jnp.exp2(best[r] - new) + pv(p, values(j))
            best[r] = new
    keep = lax.broadcasted_iota(jnp.int32, (ROWS, HD), 0) < live
    for r in range(parts):
        out = accum[r][:, :HD] / accum[r][:, HD:]
        for h in range(RS // ROWS):
            n = r * (RS // ROWS) + h
            o_ref[:, n * HD:(n + 1) * HD] = jnp.where(keep, out[h * ROWS:(h + 1) * ROWS], 0.0).astype(BF16)


def attend_group(shifts, place, q_ref, sk_ref, sv_ref, k_ref, v_ref, out_refs):
    for shift, o_ref in zip(shifts, out_refs):
        t = lax.rem(place[1] + shift, 8)
        attend(t, place[3] - t * ROWS, q_ref, sk_ref, sv_ref, k_ref, v_ref, o_ref)


def first_kernel(shifts, place, page_map, q_ref, sk_ref, sv_ref, buf_ref, k_ref, v_ref, *out_refs):
    prepare(place, page_map, buf_ref, sk_ref, k_ref, v_ref)
    attend_group(shifts, place, q_ref, sk_ref, sv_ref, k_ref, v_ref, out_refs)


def later_kernel(shifts, place, q_ref, sk_ref, sv_ref, k_ref, v_ref, *refs):
    attend_group(shifts, place, q_ref, sk_ref, sv_ref, k_ref, v_ref, refs[-len(shifts):])


def gather_kernel(place, *refs):
    out_ref = refs[-1]
    for block, shift in zip(refs, sum(GROUPS, ())):
        source = lax.rem(place[1] + 8 - shift, 8)
        out_ref[0, :, pl.ds(pl.multiple_of(source * WIDTH, WIDTH), WIDTH)] = block[...]


def local(queries, suffix_keys, suffix_values, prefix_keys, prefix_values, hit_len, suffix_len, page_map):
    request = lax.axis_index(DEVICES).astype(jnp.int32)
    me = lax.axis_index("tensor").astype(jnp.int32)
    q = queries[0].reshape(8, ROWS, WIDTH)
    sk, sv = suffix_keys[0], suffix_values[0]
    packed = jnp.concatenate([prefix_keys[0], prefix_values[0]], axis=1)
    buf = lax.all_to_all(packed, DEVICES, split_axis=0, concat_axis=0, tiled=True)
    place = jnp.stack([request, me, hit_len[request], suffix_len[request]])
    block = jax.ShapeDtypeStruct((ROWS, WIDTH), BF16)
    keys = [jax.ShapeDtypeStruct((KEYS, HD), BF16), jax.ShapeDtypeStruct((KEYS, 2 * HD), BF16)]
    k, v, *blocks = pl.pallas_call(
        functools.partial(first_kernel, GROUPS[0]),
        in_specs=[SMEM, SMEM] + [VMEM] * 4,
        out_specs=[VMEM] * (2 + len(GROUPS[0])),
        out_shape=keys + [block] * len(GROUPS[0]),
        compiler_params=PARAMS,
        name="attend_first",
    )(place, page_map, q, sk, sv, buf)
    def send(blocks, shifts):
        return [
            lax.ppermute(x, "tensor", [(z, (z + d) % 8) for z in range(8)]) if d else x
            for x, d in zip(blocks, shifts)
        ]

    sent = [send(blocks, GROUPS[0])]
    for i, shifts in enumerate(GROUPS[1:]):
        arrived = sent[i - 1] if i else []
        blocks = pl.pallas_call(
            functools.partial(later_kernel, shifts),
            in_specs=[SMEM] + [VMEM] * 5 + [pl.BlockSpec(memory_space=pl.ANY)] * len(arrived),
            out_specs=[VMEM] * len(shifts),
            out_shape=[block] * len(shifts),
            compiler_params=PARAMS,
            name="attend_later",
        )(place, q, sk, sv, k, v, *arrived)
        sent.append(send(blocks, shifts))
    blocks = sum(sent, [])
    return pl.pallas_call(
        gather_kernel,
        in_specs=[SMEM] + [VMEM] * 8,
        out_specs=VMEM,
        out_shape=jax.ShapeDtypeStruct((1, ROWS, 8 * WIDTH), BF16),
        compiler_params=PARAMS,
        name="gather_blocks",
    )(place, *blocks)


def solution(mesh):
    placed = (
        P(DEVICES, None, "tensor"),
        P(DEVICES, None, "tensor"),
        P(DEVICES, None, "tensor"),
        P(DEVICES, None, None, "tensor"),
        P(DEVICES, None, None, "tensor"),
        P(),
        P(),
        P(),
    )
    return jax.shard_map(
        local, mesh=mesh, in_specs=placed, out_specs=P(DEVICES, "tensor", None), check_vma=False
    )
```

time: 169 us -> 86.9 us (0.51)
  matrix products: 50.2 us -> 0 us
  blocking collectives: 35.8 us -> 0 us
  other arithmetic: 32.7 us -> 4.48 us
  Pallas kernels: 0 us -> 26.1 us
  local copies, waits for them, and re-layouts: 15.4 us -> 1.28 us
  starting transfers between devices: 13.4 us -> 26.5 us
  waiting for transfers between devices: 20.2 us -> 27.3 us
    dot_general x18 -> x0, matrix products: 50.2 us -> none  [the longest x9 37.4 us: block_update(): jnp.einsum('xmar,rxo->xmao', attention_weights, value_tile_rows, preferre...]
    all_to_all x1 -> x0, blocking collectives: 35.8 us -> none  [local(): lax.all_to_all(result, 'tensor', split_axis=1, concat_axis=2, tiled=True)]
    pallas_call x0 -> x4, Pallas kernels: none -> 26.1 us  [the longest x2 14.8 us: local(): pl.pallas_call(functools.partial(later_kernel, shifts), in_specs=[SMEM] +...]
    reduce_sum x10 -> x0, other arithmetic: 19 us -> none  [the longest x9 18.9 us: block_update(): row_total = row_total * shrink + jnp.sum(exp_weights, axis=-1)]
    ppermute x0 -> x7, starting transfers between devices: none -> 17.8 us  [send(): lax.ppermute(x, 'tensor', [(z, (z + d) % 8) for z in range(8)])]
    unnamed x1 -> x0, other arithmetic: 6.79 us -> none
    lt x9 -> x0, other arithmetic: 6.35 us -> none  [the longest x8 5.7 us: visit(): lax.dynamic_slice_in_dim(key_position, block_offset, keys_in_block, 0)]
    unnamed x18 -> x12, local copies, waits for them, and re-layouts: 5.16 us -> 0.03 us
  transfers between devices with their start and end apart: 2 -> 8, of which waited for: 2 -> 2; matrix products, arithmetic and copies ran while one was open for 8% -> 3% of each run, Pallas kernels for 0% -> 17%
where the time goes in v1:
time: 86.9 us; the launch traced here: 85.8 us
  waiting for transfers between devices  27.3 us (31%)
  starting transfers between devices  26.5 us (30%)
  Pallas kernels  26.1 us (30%)
  other arithmetic  4.48 us (5%)
  local copies, waits for them, and re-layouts  1.28 us (1%)
    all_to_all x1, waiting for transfers between devices, local(): lax.all_to_all(packed, DEVICES, split_axis=0, concat_axis=0, tiled=True)  25.2 us
    ppermute x7, starting transfers between devices, send(): lax.ppermute(x, 'tensor', [(z, (z + d) % 8) for z in range(8)])  17.8 us
    pallas_call x2, Pallas kernels, local(): pl.pallas_call(functools.partial(later_kernel, shifts), in_specs=[SMEM] +...  14.8 us
    pallas_call x1, Pallas kernels, local(): pl.pallas_call(functools.partial(first_kernel, GROUPS[0]), in_specs=[SMEM...  9.78 us
    all_to_all x1, starting transfers between devices, local(): lax.all_to_all(packed, DEVICES, split_axis=0, concat_axis=0, tiled=True)  8.74 us
    concatenate x1, other arithmetic, local(): packed = jnp.concatenate([prefix_keys[0], prefix_values[0]], axis=1)  3.1 us
    ppermute x7, waiting for transfers between devices, send(): lax.ppermute(x, 'tensor', [(z, (z + d) % 8) for z in range(8)])  2.08 us
  transfers between devices with their start and end apart: 8, of which 2 were waited for; matrix products, arithmetic and copies ran while one was open for 3% of the time, Pallas kernels for 17%

profile of v1, /device:TPU:1, one launch (start us, length us, event | category | flops | bytes accessed | tf_op | source)
XLA Modules:
  0.0 85.8 jit_solution(18192084213309043461)
XLA Ops:
  0.0 3.1 %pad_maximum_fusion = bf16[32,256,128]{2,1,0:T(8,128)(2,1)} fusion(bf16[32,128,128]{2,1,0:T(8,128)(2,1)} %bitcast.16, bf16[32,128,128]{2,1,0:T(8,128)(2,1)} %bitcast.17), kind=kLoop, calls=%fused_computation | loop fusion | flops 4194304 | bytes 4194304 | tf_op jit(solution)/shard_map/concatenate | solution.py:135
  3.1 0.0 copy-start.4
  3.1 0.0 copy-start.5
  3.1 0.0 copy-start
  3.1 0.0 copy-start.1
  3.1 0.0 copy-start.2
  3.1 0.0 copy-start.3
  3.1 8.7 %all-to-all-start = ((bf16[32,256,128]{2,1,0:T(8,128)(2,1)}), bf16[32,256,128]{2,1,0:T(8,128)(2,1)S(1)}, u32[]{:S(2)}, u32[]{:S(2)}) async-start(bf16[32,256,128]{2,1,0:T(8,128)(2,1)} %pad_maximum_fusion), calls=%async_computation | async-start | bytes 4194304 | tf_op jit(solution)/shard_map/all_to_all | solution.py:136
  11.9 0.0 copy-done.4
  11.9 0.6 dynamic_slice.7
  12.5 0.0 copy-done.5
  12.5 0.7 dynamic_slice.6
  13.2 1.4 %pad_add_fusion.place = s32[4]{0:T(128)S(1)} fusion(s32[1]{0:T(128)} %dynamic_slice.7, s32[1]{0:T(128)} %dynamic_slice.6, s32[1]{0:T(128)} %bitcast.1, s32[1]{0:T(128)} %bitcast), kind=kLoop, calls=%fused_computation.1 | loop fusion | flops 12 | bytes 32 | tf_op jit(solution)/shard_map/stack | solution.py:137
  14.5 25.2 %all-to-all-done.buf_ref = bf16[32,256,128]{2,1,0:T(8,128)(2,1)S(1)} async-done(((bf16[32,256,128]{2,1,0:T(8,128)(2,1)}), bf16[32,256,128]{2,1,0:T(8,128)(2,1)S(1)}, u32[]{:S(2)}, u32[]{:S(2)}) %all-to-all-start) | async-done | bytes 2097184 | tf_op jit(solution)/shard_map/all_to_all | solution.py:136
  39.7 0.0 copy-done
  39.7 0.0 copy-done.1
  39.7 0.0 copy-done.2
  39.7 0.0 copy-done.3
  39.7 9.8 %attend_first.1 = (bf16[4096,128]{1,0:T(8,128)(2,1)S(1)}, bf16[4096,256]{1,0:T(8,128)(2,1)S(1)}, bf16[32,2048]{1,0:T(8,128)(2,1)S(1)}, bf16[32,2048]{1,0:T(8,128)(2,1)S(1)}, bf16[32,2048]{1,0:T(8,128)(2,1)S(1)}) custom-call(s32[4]{0:T(128)S(1)} %pad_add_fusion.place, s32[32,32]{1,0:T(8,128)S(1)} %copy-done.3, bf16[8,32,2048]{2,1,0:T(8,128)(2,1)S(1)} %bitcast.7, ...), custom_call_target="tpu_custom_call" | custom-call | tf_op jit(solution)/shard_map/attend_first/pallas_call | solution.py:140
  49.5 7.0 %collective-permute-start = (bf16[32,2048]{1,0:T(8,128)(2,1)S(1)}, bf16[32,2048]{1,0:T(8,128)(2,1)S(1)}, u32[]{:S(2)}, u32[]{:S(2)}) collective-permute-start(bf16[32,2048]{1,0:T(8,128)(2,1)S(1)} %get-tuple-element.14), channel_id=1, source_target_pairs={{0,4},{1,5},{2,6},{3,7},{4,0},{5,1},{6,2},{7,3},{8,12},{9,13},{10,... | collective-permute-start | bytes 393224 | tf_op jit(solution)/shard_map/ppermute | solution.py:150
  56.5 1.6 %collective-permute-start.1 = (bf16[32,2048]{1,0:T(8,128)(2,1)S(1)}, bf16[32,2048]{1,0:T(8,128)(2,1)S(1)}, u32[]{:S(2)}, u32[]{:S(2)}) collective-permute-start(bf16[32,2048]{1,0:T(8,128)(2,1)S(1)} %get-tuple-element.15), channel_id=1, source_target_pairs={{0,3},{1,4},{2,5},{3,6},{4,7},{5,0},{6,1},{7,2},{8,11},{9,12},{10,... | collective-permute-start | bytes 393224 | tf_op jit(solution)/shard_map/ppermute | solution.py:150
  58.2 2.8 %collective-permute-start.2 = (bf16[32,2048]{1,0:T(8,128)(2,1)S(1)}, bf16[32,2048]{1,0:T(8,128)(2,1)S(1)}, u32[]{:S(2)}, u32[]{:S(2)}) collective-permute-start(bf16[32,2048]{1,0:T(8,128)(2,1)S(1)} %get-tuple-element.16), channel_id=1, source_target_pairs={{0,5},{1,6},{2,7},{3,0},{4,1},{5,2},{6,3},{7,4},{8,13},{9,14},{10,... | collective-permute-start | bytes 393224 | tf_op jit(solution)/shard_map/ppermute | solution.py:150
  61.0 11.4 %attend_later.2 = (bf16[32,2048]{1,0:T(8,128)(2,1)S(1)}, bf16[32,2048]{1,0:T(8,128)(2,1)S(1)}, bf16[32,2048]{1,0:T(8,128)(2,1)S(1)}, bf16[32,2048]{1,0:T(8,128)(2,1)S(1)}) custom-call(s32[4]{0:T(128)S(1)} %pad_add_fusion.place, bf16[8,32,2048]{2,1,0:T(8,128)(2,1)S(1)} %bitcast.8, bf16[256,128]{1,0:T(8,128)(2,1)S(1)} %bitcast.11, ...), custom_call_target="tpu_custom_call" | custom-call | tf_op jit(solution)/shard_map/attend_later/pallas_call | solution.py:157
  72.4 1.3 %collective-permute-start.3 = (bf16[32,2048]{1,0:T(8,128)(2,1)S(1)}, bf16[32,2048]{1,0:T(8,128)(2,1)S(1)}, u32[]{:S(2)}, u32[]{:S(2)}) collective-permute-start(bf16[32,2048]{1,0:T(8,128)(2,1)S(1)} %get-tuple-element.19), channel_id=1, source_target_pairs={{0,2},{1,3},{2,4},{3,5},{4,6},{5,7},{6,0},{7,1},{8,10},{9,11},{10,... | collective-permute-start | bytes 393224 | tf_op jit(solution)/shard_map/ppermute | solution.py:150
  73.7 2.4 %collective-permute-start.4 = (bf16[32,2048]{1,0:T(8,128)(2,1)S(1)}, bf16[32,2048]{1,0:T(8,128)(2,1)S(1)}, u32[]{:S(2)}, u32[]{:S(2)}) collective-permute-start(bf16[32,2048]{1,0:T(8,128)(2,1)S(1)} %get-tuple-element.20), channel_id=1, source_target_pairs={{0,6},{1,7},{2,0},{3,1},{4,2},{5,3},{6,4},{7,5},{8,14},{9,15},{10,... | collective-permute-start | bytes 393224 | tf_op jit(solution)/shard_map/ppermute | solution.py:150
  76.1 0.0 collective-permute-done.refs_0_
  76.1 0.7 collective-permute-start.5
  76.8 0.0 collective-permute-done.1.refs_1_
  76.8 1.9 %collective-permute-start.6 = (bf16[32,2048]{1,0:T(8,128)(2,1)S(1)}, bf16[32,2048]{1,0:T(8,128)(2,1)S(1)}, u32[]{:S(2)}, u32[]{:S(2)}) collective-permute-start(bf16[32,2048]{1,0:T(8,128)(2,1)S(1)} %get-tuple-element.22), channel_id=1, source_target_pairs={{0,7},{1,0},{2,1},{3,2},{4,3},{5,4},{6,5},{7,6},{8,15},{9,8},{10,9... | collective-permute-start | bytes 393224 | tf_op jit(solution)/shard_map/ppermute | solution.py:150
  78.7 0.0 collective-permute-done.2.refs_2_
  78.8 3.4 %attend_later.3.refs_7_ = bf16[32,2048]{1,0:T(8,128)(2,1)S(1)} custom-call(s32[4]{0:T(128)S(1)} %pad_add_fusion.place, bf16[8,32,2048]{2,1,0:T(8,128)(2,1)S(1)} %bitcast.9, bf16[256,128]{1,0:T(8,128)(2,1)S(1)} %bitcast.12, bf16[256,128]{1,0:T(8,128)(2,1)S(1)} %bitcast.15, bf16[4096,128]{1,0:T(8,128)(2,1)S(1)} %get-tuple-element.17.k_ref, ...), custom_call_target="tpu_custom_call" | custom-call | tf_op jit(solution)/shard_map/attend_later/pallas_call | solution.py:157
  82.1 0.0 collective-permute-done.3.refs_3_
  82.1 0.0 collective-permute-done.4.refs_4_
  82.1 2.1 %collective-permute-done.5.refs_5_ = bf16[32,2048]{1,0:T(8,128)(2,1)S(1)} collective-permute-done((bf16[32,2048]{1,0:T(8,128)(2,1)S(1)}, bf16[32,2048]{1,0:T(8,128)(2,1)S(1)}, u32[]{:S(2)}, u32[]{:S(2)}) %collective-permute-start.5) | collective-permute-done | bytes 131104 | tf_op jit(solution)/shard_map/ppermute | solution.py:150
  84.2 0.0 collective-permute-done.6.refs_6_
  84.2 1.6 %gather_blocks.1 = bf16[1,32,16384]{2,1,0:T(8,128)(2,1)} custom-call(s32[4]{0:T(128)S(1)} %pad_add_fusion.place, bf16[32,2048]{1,0:T(8,128)(2,1)S(1)} %collective-permute-done.refs_0_, bf16[32,2048]{1,0:T(8,128)(2,1)S(1)} %collective-permute-done.1.refs_1_, bf16[32,2048]{1,0:T(8,128)(2,1)S(1)} %collective-permute-done.2.refs_2_, ...), custom_call_target="tpu_custom_call" | custom-call | tf_op jit(solution)/shard_map/gather_blocks/pallas_call | solution.py:167
Async XLA Ops:
  3.1 8.8 %copy-start.4 = (s32[32]{0:T(128)S(1)}, s32[32]{0:T(128)}, u32[]{:S(2)}) copy-start(s32[32]{0:T(128)} %param.14) | copy-start | bytes 388
  3.1 9.4 %copy-start.5 = (s32[32]{0:T(128)S(1)}, s32[32]{0:T(128)}, u32[]{:S(2)}) copy-start(s32[32]{0:T(128)} %param.13) | copy-start | bytes 388
  3.1 36.6 %copy-start = (bf16[1,256,2048]{2,1,0:T(8,128)(2,1)S(1)}, bf16[1,256,2048]{2,1,0:T(8,128)(2,1)}, u32[]{:S(2)}) copy-start(bf16[1,256,2048]{2,1,0:T(8,128)(2,1)} %param.8) | copy-start | bytes 3145732
  3.1 36.6 %copy-start.1 = (bf16[1,256,128]{2,1,0:T(8,128)(2,1)S(1)}, bf16[1,256,128]{2,1,0:T(8,128)(2,1)}, u32[]{:S(2)}) copy-start(bf16[1,256,128]{2,1,0:T(8,128)(2,1)} %param.9) | copy-start | bytes 196612
  3.1 36.6 %copy-start.2 = (bf16[1,256,128]{2,1,0:T(8,128)(2,1)S(1)}, bf16[1,256,128]{2,1,0:T(8,128)(2,1)}, u32[]{:S(2)}) copy-start(bf16[1,256,128]{2,1,0:T(8,128)(2,1)} %param.10) | copy-start | bytes 196612
  3.1 36.6 %copy-start.3 = (s32[32,32]{1,0:T(8,128)S(1)}, s32[32,32]{1,0:T(8,128)}, u32[]{:S(2)}) copy-start(s32[32,32]{1,0:T(8,128)} %page_map.1) | copy-start | bytes 12292
  3.1 36.6 %all-to-all-start = ((bf16[32,256,128]{2,1,0:T(8,128)(2,1)}), bf16[32,256,128]{2,1,0:T(8,128)(2,1)S(1)}, u32[]{:S(2)}, u32[]{:S(2)}) async-start(bf16[32,256,128]{2,1,0:T(8,128)(2,1)} %pad_maximum_fusion), calls=%async_computation | async-start | bytes 4194304 | tf_op jit(solution)/shard_map/all_to_all | solution.py:136
  49.5 26.5 %collective-permute-start = (bf16[32,2048]{1,0:T(8,128)(2,1)S(1)}, bf16[32,2048]{1,0:T(8,128)(2,1)S(1)}, u32[]{:S(2)}, u32[]{:S(2)}) collective-permute-start(bf16[32,2048]{1,0:T(8,128)(2,1)S(1)} %get-tuple-element.14), channel_id=1, source_target_pairs={{0,4},{1,5},{2,6},{3,7},{4,0},{5,1},{6,2},{7,3},{8,12},{9,13},{10,... | collective-permute-start | bytes 393224 | tf_op jit(solution)/shard_map/ppermute | solution.py:150
  56.5 20.3 %collective-permute-start.1 = (bf16[32,2048]{1,0:T(8,128)(2,1)S(1)}, bf16[32,2048]{1,0:T(8,128)(2,1)S(1)}, u32[]{:S(2)}, u32[]{:S(2)}) collective-permute-start(bf16[32,2048]{1,0:T(8,128)(2,1)S(1)} %get-tuple-element.15), channel_id=1, source_target_pairs={{0,3},{1,4},{2,5},{3,6},{4,7},{5,0},{6,1},{7,2},{8,11},{9,12},{10,... | collective-permute-start | bytes 393224 | tf_op jit(solution)/shard_map/ppermute | solution.py:150
  58.2 20.6 %collective-permute-start.2 = (bf16[32,2048]{1,0:T(8,128)(2,1)S(1)}, bf16[32,2048]{1,0:T(8,128)(2,1)S(1)}, u32[]{:S(2)}, u32[]{:S(2)}) collective-permute-start(bf16[32,2048]{1,0:T(8,128)(2,1)S(1)} %get-tuple-element.16), channel_id=1, source_target_pairs={{0,5},{1,6},{2,7},{3,0},{4,1},{5,2},{6,3},{7,4},{8,13},{9,14},{10,... | collective-permute-start | bytes 393224 | tf_op jit(solution)/shard_map/ppermute | solution.py:150
  72.4 9.7 %collective-permute-start.3 = (bf16[32,2048]{1,0:T(8,128)(2,1)S(1)}, bf16[32,2048]{1,0:T(8,128)(2,1)S(1)}, u32[]{:S(2)}, u32[]{:S(2)}) collective-permute-start(bf16[32,2048]{1,0:T(8,128)(2,1)S(1)} %get-tuple-element.19), channel_id=1, source_target_pairs={{0,2},{1,3},{2,4},{3,5},{4,6},{5,7},{6,0},{7,1},{8,10},{9,11},{10,... | collective-permute-start | bytes 393224 | tf_op jit(solution)/shard_map/ppermute | solution.py:150
  73.7 8.4 %collective-permute-start.4 = (bf16[32,2048]{1,0:T(8,128)(2,1)S(1)}, bf16[32,2048]{1,0:T(8,128)(2,1)S(1)}, u32[]{:S(2)}, u32[]{:S(2)}) collective-permute-start(bf16[32,2048]{1,0:T(8,128)(2,1)S(1)} %get-tuple-element.20), channel_id=1, source_target_pairs={{0,6},{1,7},{2,0},{3,1},{4,2},{5,3},{6,4},{7,5},{8,14},{9,15},{10,... | collective-permute-start | bytes 393224 | tf_op jit(solution)/shard_map/ppermute | solution.py:150
  76.1 8.1 %collective-permute-start.5 = (bf16[32,2048]{1,0:T(8,128)(2,1)S(1)}, bf16[32,2048]{1,0:T(8,128)(2,1)S(1)}, u32[]{:S(2)}, u32[]{:S(2)}) collective-permute-start(bf16[32,2048]{1,0:T(8,128)(2,1)S(1)} %get-tuple-element.21), channel_id=1, source_target_pairs={{0,1},{1,2},{2,3},{3,4},{4,5},{5,6},{6,7},{7,0},{8,9},{9,10},{10,1... | collective-permute-start | bytes 393224 | tf_op jit(solution)/shard_map/ppermute | solution.py:150
  76.8 7.4 %collective-permute-start.6 = (bf16[32,2048]{1,0:T(8,128)(2,1)S(1)}, bf16[32,2048]{1,0:T(8,128)(2,1)S(1)}, u32[]{:S(2)}, u32[]{:S(2)}) collective-permute-start(bf16[32,2048]{1,0:T(8,128)(2,1)S(1)} %get-tuple-element.22), channel_id=1, source_target_pairs={{0,7},{1,0},{2,1},{3,2},{4,3},{5,4},{6,5},{7,6},{8,15},{9,8},{10,9... | collective-permute-start | bytes 393224 | tf_op jit(solution)/shard_map/ppermute | solution.py:150

commit v2 on v1

--- a/solution.py
+++ b/solution.py
@@ -19,7 +19,7 @@
 RB = ROWS * HEADS
 TILE = 1024
 RS = 512
-GROUPS = ((4, 3, 5), (2, 6, 1, 7), (0,))
+GROUPS = ((4, 5, 3), (6, 2, 7, 1), (0,))
 SCALE = math.log2(math.e) / math.sqrt(HD)
 F32 = jnp.float32
 BF16 = jnp.bfloat16
@@ -38,20 +38,32 @@
 
 
 def prepare(place, page_map, buf_ref, sk_ref, k_out, v_out):
-    first_key = sk_ref[0:1, :].astype(F32)
-    slot = lax.broadcasted_iota(jnp.int32, (PAGE, HD), 0)
     request, hit = place[0], place[2]
 
-    def page(p, _):
+    def page(p, whole):
         holder = page_map[request, p]
-        valid = slot < hit - p * PAGE
         rows = pl.ds(pl.multiple_of(p * PAGE, PAGE), PAGE)
-        k_out[rows, :] = jnp.where(valid, buf_ref[holder, :PAGE, :].astype(F32), first_key).astype(BF16)
-        v_out[rows, :HD] = jnp.where(valid, buf_ref[holder, PAGE:, :].astype(F32), 0.0).astype(BF16)
-        v_out[rows, HD:] = jnp.where(valid, 1.0, 0.0).astype(BF16)
+        if whole:
+            k_out[rows, :] = buf_ref[holder, :PAGE, :]
+            v_out[rows, :HD] = buf_ref[holder, PAGE:, :]
+            v_out[rows, HD:] = jnp.ones((PAGE, HD), BF16)
+        else:
+            valid = lax.broadcasted_iota(jnp.int32, (PAGE, HD), 0) < hit - p * PAGE
+            k, v = buf_ref[holder, :PAGE, :].astype(F32), buf_ref[holder, PAGE:, :].astype(F32)
+            k_out[rows, :] = jnp.where(valid, k, sk_ref[0:1, :].astype(F32)).astype(BF16)
+            v_out[rows, :HD] = jnp.where(valid, v, 0.0).astype(BF16)
+            v_out[rows, HD:] = jnp.where(valid, 1.0, 0.0).astype(BF16)
+
+    def tile(j, _):
+        for whole in (True, False):
+            @pl.when((hit >= (j + 1) * TILE) == whole)
+            def _(whole=whole):
+                for i in range(TILE // PAGE):
+                    page(j * (TILE // PAGE) + i, whole)
+
         return 0
 
-    lax.fori_loop(0, PAGES, page, 0, unroll=4)
+    lax.fori_loop(0, KEYS // TILE, tile, 0)
 
 
 def row_block(q_ref, t):

time: 86.9 us -> 85.8 us (0.987)
  starting transfers between devices: 26.5 us -> 23.7 us
  waiting for transfers between devices: 27.3 us -> 28.5 us
    ppermute x7, starting transfers between devices: 17.8 us -> 15 us  [send(): lax.ppermute(x, 'tensor', [(z, (z + d) % 8) for z in range(8)])]
    ppermute x7, waiting for transfers between devices: 2.08 us -> 3.3 us  [send(): lax.ppermute(x, 'tensor', [(z, (z + d) % 8) for z in range(8)])]
  transfers between devices with their start and end apart: 8 -> 8, of which waited for: 2 -> 3; matrix products, arithmetic and copies ran while one was open for 3% -> 3% of each run, Pallas kernels for 17% -> 18%
where the time goes in v2:
time: 85.8 us; the launch traced here: 84.3 us
  waiting for transfers between devices  28.5 us (33%)
  Pallas kernels  26.2 us (31%)
  starting transfers between devices  23.7 us (28%)
  other arithmetic  4.48 us (5%)
  local copies, waits for them, and re-layouts  1.28 us (1%)
    all_to_all x1, waiting for transfers between devices, local(): lax.all_to_all(packed, DEVICES, split_axis=0, concat_axis=0, tiled=True)  25.2 us
    ppermute x7, starting transfers between devices, send(): lax.ppermute(x, 'tensor', [(z, (z + d) % 8) for z in range(8)])  15 us
    pallas_call x2, Pallas kernels, local(): pl.pallas_call(functools.partial(later_kernel, shifts), in_specs=[SMEM] +...  14.8 us
    pallas_call x1, Pallas kernels, local(): pl.pallas_call(functools.partial(first_kernel, GROUPS[0]), in_specs=[SMEM...  9.86 us
    all_to_all x1, starting transfers between devices, local(): lax.all_to_all(packed, DEVICES, split_axis=0, concat_axis=0, tiled=True)  8.74 us
    ppermute x7, waiting for transfers between devices, send(): lax.ppermute(x, 'tensor', [(z, (z + d) % 8) for z in range(8)])  3.3 us
    concatenate x1, other arithmetic, local(): packed = jnp.concatenate([prefix_keys[0], prefix_values[0]], axis=1)  3.1 us
  transfers between devices with their start and end apart: 8, of which 3 were waited for; matrix products, arithmetic and copies ran while one was open for 3% of the time, Pallas kernels for 18%

profile of v2, /device:TPU:1, one launch (start us, length us, event | category | flops | bytes accessed | tf_op | source)
XLA Modules:
  0.0 84.3 jit_solution(8600286187861473671)
XLA Ops:
  0.0 3.1 %pad_maximum_fusion = bf16[32,256,128]{2,1,0:T(8,128)(2,1)} fusion(bf16[32,128,128]{2,1,0:T(8,128)(2,1)} %bitcast.16, bf16[32,128,128]{2,1,0:T(8,128)(2,1)} %bitcast.17), kind=kLoop, calls=%fused_computation | loop fusion | flops 4194304 | bytes 4194304 | tf_op jit(solution)/shard_map/concatenate | solution.py:147
  3.1 0.0 copy-start.4
  3.1 0.0 copy-start.5
  3.1 0.0 copy-start
  3.1 0.0 copy-start.1
  3.1 0.0 copy-start.2
  3.1 0.0 copy-start.3
  3.1 8.7 %all-to-all-start = ((bf16[32,256,128]{2,1,0:T(8,128)(2,1)}), bf16[32,256,128]{2,1,0:T(8,128)(2,1)S(1)}, u32[]{:S(2)}, u32[]{:S(2)}) async-start(bf16[32,256,128]{2,1,0:T(8,128)(2,1)} %pad_maximum_fusion), calls=%async_computation | async-start | bytes 4194304 | tf_op jit(solution)/shard_map/all_to_all | solution.py:148
  11.9 0.0 copy-done.4
  11.9 0.6 dynamic_slice.7
  12.5 0.0 copy-done.5
  12.5 0.7 dynamic_slice.6
  13.2 1.4 %pad_add_fusion.place = s32[4]{0:T(128)S(1)} fusion(s32[1]{0:T(128)} %dynamic_slice.7, s32[1]{0:T(128)} %dynamic_slice.6, s32[1]{0:T(128)} %bitcast.1, s32[1]{0:T(128)} %bitcast), kind=kLoop, calls=%fused_computation.1 | loop fusion | flops 12 | bytes 32 | tf_op jit(solution)/shard_map/stack | solution.py:149
  14.5 25.2 %all-to-all-done.buf_ref = bf16[32,256,128]{2,1,0:T(8,128)(2,1)S(1)} async-done(((bf16[32,256,128]{2,1,0:T(8,128)(2,1)}), bf16[32,256,128]{2,1,0:T(8,128)(2,1)S(1)}, u32[]{:S(2)}, u32[]{:S(2)}) %all-to-all-start) | async-done | bytes 2097184 | tf_op jit(solution)/shard_map/all_to_all | solution.py:148
  39.7 0.0 copy-done
  39.7 0.0 copy-done.1
  39.7 0.0 copy-done.2
  39.7 0.0 copy-done.3
  39.7 9.9 %attend_first.1 = (bf16[4096,128]{1,0:T(8,128)(2,1)S(1)}, bf16[4096,256]{1,0:T(8,128)(2,1)S(1)}, bf16[32,2048]{1,0:T(8,128)(2,1)S(1)}, bf16[32,2048]{1,0:T(8,128)(2,1)S(1)}, bf16[32,2048]{1,0:T(8,128)(2,1)S(1)}) custom-call(s32[4]{0:T(128)S(1)} %pad_add_fusion.place, s32[32,32]{1,0:T(8,128)S(1)} %copy-done.3, bf16[8,32,2048]{2,1,0:T(8,128)(2,1)S(1)} %bitcast.7, ...), custom_call_target="tpu_custom_call" | custom-call | tf_op jit(solution)/shard_map/attend_first/pallas_call | solution.py:152
  49.6 7.0 %collective-permute-start = (bf16[32,2048]{1,0:T(8,128)(2,1)S(1)}, bf16[32,2048]{1,0:T(8,128)(2,1)S(1)}, u32[]{:S(2)}, u32[]{:S(2)}) collective-permute-start(bf16[32,2048]{1,0:T(8,128)(2,1)S(1)} %get-tuple-element.14), channel_id=1, source_target_pairs={{0,4},{1,5},{2,6},{3,7},{4,0},{5,1},{6,2},{7,3},{8,12},{9,13},{10,... | collective-permute-start | bytes 393224 | tf_op jit(solution)/shard_map/ppermute | solution.py:162
  56.6 0.0 collective-permute-start.1
  56.6 3.3 %collective-permute-start.2 = (bf16[32,2048]{1,0:T(8,128)(2,1)S(1)}, bf16[32,2048]{1,0:T(8,128)(2,1)S(1)}, u32[]{:S(2)}, u32[]{:S(2)}) collective-permute-start(bf16[32,2048]{1,0:T(8,128)(2,1)S(1)} %get-tuple-element.16), channel_id=1, source_target_pairs={{0,3},{1,4},{2,5},{3,6},{4,7},{5,0},{6,1},{7,2},{8,11},{9,12},{10,... | collective-permute-start | bytes 393224 | tf_op jit(solution)/shard_map/ppermute | solution.py:162
  59.9 11.4 %attend_later.2 = (bf16[32,2048]{1,0:T(8,128)(2,1)S(1)}, bf16[32,2048]{1,0:T(8,128)(2,1)S(1)}, bf16[32,2048]{1,0:T(8,128)(2,1)S(1)}, bf16[32,2048]{1,0:T(8,128)(2,1)S(1)}) custom-call(s32[4]{0:T(128)S(1)} %pad_add_fusion.place, bf16[8,32,2048]{2,1,0:T(8,128)(2,1)S(1)} %bitcast.8, bf16[256,128]{1,0:T(8,128)(2,1)S(1)} %bitcast.11, ...), custom_call_target="tpu_custom_call" | custom-call | tf_op jit(solution)/shard_map/attend_later/pallas_call | solution.py:169
  71.3 0.8 %collective-permute-start.3 = (bf16[32,2048]{1,0:T(8,128)(2,1)S(1)}, bf16[32,2048]{1,0:T(8,128)(2,1)S(1)}, u32[]{:S(2)}, u32[]{:S(2)}) collective-permute-start(bf16[32,2048]{1,0:T(8,128)(2,1)S(1)} %get-tuple-element.19), channel_id=1, source_target_pairs={{0,6},{1,7},{2,0},{3,1},{4,2},{5,3},{6,4},{7,5},{8,14},{9,15},{10,... | collective-permute-start | bytes 393224 | tf_op jit(solution)/shard_map/ppermute | solution.py:162
  72.1 1.9 %collective-permute-start.4 = (bf16[32,2048]{1,0:T(8,128)(2,1)S(1)}, bf16[32,2048]{1,0:T(8,128)(2,1)S(1)}, u32[]{:S(2)}, u32[]{:S(2)}) collective-permute-start(bf16[32,2048]{1,0:T(8,128)(2,1)S(1)} %get-tuple-element.20), channel_id=1, source_target_pairs={{0,2},{1,3},{2,4},{3,5},{4,6},{5,7},{6,0},{7,1},{8,10},{9,11},{10,... | collective-permute-start | bytes 393224 | tf_op jit(solution)/shard_map/ppermute | solution.py:162
  74.1 0.0 collective-permute-done.refs_0_
  74.1 1.9 %collective-permute-start.5 = (bf16[32,2048]{1,0:T(8,128)(2,1)S(1)}, bf16[32,2048]{1,0:T(8,128)(2,1)S(1)}, u32[]{:S(2)}, u32[]{:S(2)}) collective-permute-start(bf16[32,2048]{1,0:T(8,128)(2,1)S(1)} %get-tuple-element.21), channel_id=1, source_target_pairs={{0,7},{1,0},{2,1},{3,2},{4,3},{5,4},{6,5},{7,6},{8,15},{9,8},{10,9... | collective-permute-start | bytes 393224 | tf_op jit(solution)/shard_map/ppermute | solution.py:162
  76.0 0.0 collective-permute-done.1.refs_1_
  76.0 0.0 collective-permute-start.6
  76.0 0.0 collective-permute-done.2.refs_2_
  76.0 3.4 %attend_later.3.refs_7_ = bf16[32,2048]{1,0:T(8,128)(2,1)S(1)} custom-call(s32[4]{0:T(128)S(1)} %pad_add_fusion.place, bf16[8,32,2048]{2,1,0:T(8,128)(2,1)S(1)} %bitcast.9, bf16[256,128]{1,0:T(8,128)(2,1)S(1)} %bitcast.12, bf16[256,128]{1,0:T(8,128)(2,1)S(1)} %bitcast.15, bf16[4096,128]{1,0:T(8,128)(2,1)S(1)} %get-tuple-element.17.k_ref, ...), custom_call_target="tpu_custom_call" | custom-call | tf_op jit(solution)/shard_map/attend_later/pallas_call | solution.py:169
  79.4 0.0 collective-permute-done.3.refs_3_
  79.4 0.0 collective-permute-done.4.refs_4_
  79.4 1.2 %collective-permute-done.5.refs_5_ = bf16[32,2048]{1,0:T(8,128)(2,1)S(1)} collective-permute-done((bf16[32,2048]{1,0:T(8,128)(2,1)S(1)}, bf16[32,2048]{1,0:T(8,128)(2,1)S(1)}, u32[]{:S(2)}, u32[]{:S(2)}) %collective-permute-start.5) | collective-permute-done | bytes 131104 | tf_op jit(solution)/shard_map/ppermute | solution.py:162
  80.6 2.1 %collective-permute-done.6.refs_6_ = bf16[32,2048]{1,0:T(8,128)(2,1)S(1)} collective-permute-done((bf16[32,2048]{1,0:T(8,128)(2,1)S(1)}, bf16[32,2048]{1,0:T(8,128)(2,1)S(1)}, u32[]{:S(2)}, u32[]{:S(2)}) %collective-permute-start.6) | collective-permute-done | bytes 131104 | tf_op jit(solution)/shard_map/ppermute | solution.py:162
  82.7 1.6 %gather_blocks.1 = bf16[1,32,16384]{2,1,0:T(8,128)(2,1)} custom-call(s32[4]{0:T(128)S(1)} %pad_add_fusion.place, bf16[32,2048]{1,0:T(8,128)(2,1)S(1)} %collective-permute-done.refs_0_, bf16[32,2048]{1,0:T(8,128)(2,1)S(1)} %collective-permute-done.1.refs_1_, bf16[32,2048]{1,0:T(8,128)(2,1)S(1)} %collective-permute-done.2.refs_2_, ...), custom_call_target="tpu_custom_call" | custom-call | tf_op jit(solution)/shard_map/gather_blocks/pallas_call | solution.py:179
Async XLA Ops:
  3.1 8.8 %copy-start.4 = (s32[32]{0:T(128)S(1)}, s32[32]{0:T(128)}, u32[]{:S(2)}) copy-start(s32[32]{0:T(128)} %param.14) | copy-start | bytes 388
  3.1 9.4 %copy-start.5 = (s32[32]{0:T(128)S(1)}, s32[32]{0:T(128)}, u32[]{:S(2)}) copy-start(s32[32]{0:T(128)} %param.13) | copy-start | bytes 388
  3.1 36.6 %copy-start = (bf16[1,256,2048]{2,1,0:T(8,128)(2,1)S(1)}, bf16[1,256,2048]{2,1,0:T(8,128)(2,1)}, u32[]{:S(2)}) copy-start(bf16[1,256,2048]{2,1,0:T(8,128)(2,1)} %param.8) | copy-start | bytes 3145732
  3.1 36.6 %copy-start.1 = (bf16[1,256,128]{2,1,0:T(8,128)(2,1)S(1)}, bf16[1,256,128]{2,1,0:T(8,128)(2,1)}, u32[]{:S(2)}) copy-start(bf16[1,256,128]{2,1,0:T(8,128)(2,1)} %param.9) | copy-start | bytes 196612
  3.1 36.6 %copy-start.2 = (bf16[1,256,128]{2,1,0:T(8,128)(2,1)S(1)}, bf16[1,256,128]{2,1,0:T(8,128)(2,1)}, u32[]{:S(2)}) copy-start(bf16[1,256,128]{2,1,0:T(8,128)(2,1)} %param.10) | copy-start | bytes 196612
  3.1 36.6 %copy-start.3 = (s32[32,32]{1,0:T(8,128)S(1)}, s32[32,32]{1,0:T(8,128)}, u32[]{:S(2)}) copy-start(s32[32,32]{1,0:T(8,128)} %page_map.1) | copy-start | bytes 12292
  3.1 36.6 %all-to-all-start = ((bf16[32,256,128]{2,1,0:T(8,128)(2,1)}), bf16[32,256,128]{2,1,0:T(8,128)(2,1)S(1)}, u32[]{:S(2)}, u32[]{:S(2)}) async-start(bf16[32,256,128]{2,1,0:T(8,128)(2,1)} %pad_maximum_fusion), calls=%async_computation | async-start | bytes 4194304 | tf_op jit(solution)/shard_map/all_to_all | solution.py:148
  49.6 24.5 %collective-permute-start = (bf16[32,2048]{1,0:T(8,128)(2,1)S(1)}, bf16[32,2048]{1,0:T(8,128)(2,1)S(1)}, u32[]{:S(2)}, u32[]{:S(2)}) collective-permute-start(bf16[32,2048]{1,0:T(8,128)(2,1)S(1)} %get-tuple-element.14), channel_id=1, source_target_pairs={{0,4},{1,5},{2,6},{3,7},{4,0},{5,1},{6,2},{7,3},{8,12},{9,13},{10,... | collective-permute-start | bytes 393224 | tf_op jit(solution)/shard_map/ppermute | solution.py:162
  56.6 19.4 %collective-permute-start.1 = (bf16[32,2048]{1,0:T(8,128)(2,1)S(1)}, bf16[32,2048]{1,0:T(8,128)(2,1)S(1)}, u32[]{:S(2)}, u32[]{:S(2)}) collective-permute-start(bf16[32,2048]{1,0:T(8,128)(2,1)S(1)} %get-tuple-element.15), channel_id=1, source_target_pairs={{0,5},{1,6},{2,7},{3,0},{4,1},{5,2},{6,3},{7,4},{8,13},{9,14},{10,... | collective-permute-start | bytes 393224 | tf_op jit(solution)/shard_map/ppermute | solution.py:162
  56.6 19.4 %collective-permute-start.2 = (bf16[32,2048]{1,0:T(8,128)(2,1)S(1)}, bf16[32,2048]{1,0:T(8,128)(2,1)S(1)}, u32[]{:S(2)}, u32[]{:S(2)}) collective-permute-start(bf16[32,2048]{1,0:T(8,128)(2,1)S(1)} %get-tuple-element.16), channel_id=1, source_target_pairs={{0,3},{1,4},{2,5},{3,6},{4,7},{5,0},{6,1},{7,2},{8,11},{9,12},{10,... | collective-permute-start | bytes 393224 | tf_op jit(solution)/shard_map/ppermute | solution.py:162
  71.3 8.1 %collective-permute-start.3 = (bf16[32,2048]{1,0:T(8,128)(2,1)S(1)}, bf16[32,2048]{1,0:T(8,128)(2,1)S(1)}, u32[]{:S(2)}, u32[]{:S(2)}) collective-permute-start(bf16[32,2048]{1,0:T(8,128)(2,1)S(1)} %get-tuple-element.19), channel_id=1, source_target_pairs={{0,6},{1,7},{2,0},{3,1},{4,2},{5,3},{6,4},{7,5},{8,14},{9,15},{10,... | collective-permute-start | bytes 393224 | tf_op jit(solution)/shard_map/ppermute | solution.py:162
  72.1 7.3 %collective-permute-start.4 = (bf16[32,2048]{1,0:T(8,128)(2,1)S(1)}, bf16[32,2048]{1,0:T(8,128)(2,1)S(1)}, u32[]{:S(2)}, u32[]{:S(2)}) collective-permute-start(bf16[32,2048]{1,0:T(8,128)(2,1)S(1)} %get-tuple-element.20), channel_id=1, source_target_pairs={{0,2},{1,3},{2,4},{3,5},{4,6},{5,7},{6,0},{7,1},{8,10},{9,11},{10,... | collective-permute-start | bytes 393224 | tf_op jit(solution)/shard_map/ppermute | solution.py:162
  74.1 6.5 %collective-permute-start.5 = (bf16[32,2048]{1,0:T(8,128)(2,1)S(1)}, bf16[32,2048]{1,0:T(8,128)(2,1)S(1)}, u32[]{:S(2)}, u32[]{:S(2)}) collective-permute-start(bf16[32,2048]{1,0:T(8,128)(2,1)S(1)} %get-tuple-element.21), channel_id=1, source_target_pairs={{0,7},{1,0},{2,1},{3,2},{4,3},{5,4},{6,5},{7,6},{8,15},{9,8},{10,9... | collective-permute-start | bytes 393224 | tf_op jit(solution)/shard_map/ppermute | solution.py:162
  76.0 6.7 %collective-permute-start.6 = (bf16[32,2048]{1,0:T(8,128)(2,1)S(1)}, bf16[32,2048]{1,0:T(8,128)(2,1)S(1)}, u32[]{:S(2)}, u32[]{:S(2)}) collective-permute-start(bf16[32,2048]{1,0:T(8,128)(2,1)S(1)} %get-tuple-element.22), channel_id=1, source_target_pairs={{0,1},{1,2},{2,3},{3,4},{4,5},{5,6},{6,7},{7,0},{8,9},{9,10},{10,1... | collective-permute-start | bytes 393224 | tf_op jit(solution)/shard_map/ppermute | solution.py:162

commit v3 on v2

--- a/solution.py
+++ b/solution.py
@@ -19,7 +19,7 @@
 RB = ROWS * HEADS
 TILE = 1024
 RS = 512
-GROUPS = ((4, 5, 3), (6, 2, 7, 1), (0,))
+GROUPS = ((4, 5), (3, 6, 2), (7, 1), (0,))
 SCALE = math.log2(math.e) / math.sqrt(HD)
 F32 = jnp.float32
 BF16 = jnp.bfloat16
@@ -123,7 +123,12 @@
         attend(t, place[3] - t * ROWS, q_ref, sk_ref, sv_ref, k_ref, v_ref, o_ref)
 
 
-def first_kernel(shifts, place, page_map, q_ref, sk_ref, sv_ref, buf_ref, k_ref, v_ref, *out_refs):
+def first_kernel(shifts, hit_len, suffix_len, page_map, q_ref, sk_ref, sv_ref, buf_ref, place, k_ref, v_ref, *out_refs):
+    request = lax.axis_index("dp") * 8 + lax.axis_index("cache")
+    place[0] = request
+    place[1] = lax.axis_index("tensor")
+    place[2] = hit_len[request]
+    place[3] = suffix_len[request]
     prepare(place, page_map, buf_ref, sk_ref, k_ref, v_ref)
     attend_group(shifts, place, q_ref, sk_ref, sv_ref, k_ref, v_ref, out_refs)
 
@@ -140,23 +145,20 @@
 
 
 def local(queries, suffix_keys, suffix_values, prefix_keys, prefix_values, hit_len, suffix_len, page_map):
-    request = lax.axis_index(DEVICES).astype(jnp.int32)
-    me = lax.axis_index("tensor").astype(jnp.int32)
     q = queries[0].reshape(8, ROWS, WIDTH)
     sk, sv = suffix_keys[0], suffix_values[0]
     packed = jnp.concatenate([prefix_keys[0], prefix_values[0]], axis=1)
     buf = lax.all_to_all(packed, DEVICES, split_axis=0, concat_axis=0, tiled=True)
-    place = jnp.stack([request, me, hit_len[request], suffix_len[request]])
     block = jax.ShapeDtypeStruct((ROWS, WIDTH), BF16)
     keys = [jax.ShapeDtypeStruct((KEYS, HD), BF16), jax.ShapeDtypeStruct((KEYS, 2 * HD), BF16)]
-    k, v, *blocks = pl.pallas_call(
+    place, k, v, *blocks = pl.pallas_call(
         functools.partial(first_kernel, GROUPS[0]),
-        in_specs=[SMEM, SMEM] + [VMEM] * 4,
-        out_specs=[VMEM] * (2 + len(GROUPS[0])),
-        out_shape=keys + [block] * len(GROUPS[0]),
+        in_specs=[SMEM] * 3 + [VMEM] * 4,
+        out_specs=[SMEM] + [VMEM] * (2 + len(GROUPS[0])),
+        out_shape=[jax.ShapeDtypeStruct((4,), jnp.int32)] + keys + [block] * len(GROUPS[0]),
         compiler_params=PARAMS,
         name="attend_first",
-    )(place, page_map, q, sk, sv, buf)
+    )(hit_len, suffix_len, page_map, q, sk, sv, buf)
     def send(blocks, shifts):
         return [
             lax.ppermute(x, "tensor", [(z, (z + d) % 8) for z in range(8)]) if d else x
@@ -166,6 +168,8 @@
     sent = [send(blocks, GROUPS[0])]
     for i, shifts in enumerate(GROUPS[1:]):
         arrived = sent[i - 1] if i else []
+        if i == len(GROUPS) - 2:
+            arrived = arrived[:1]
         blocks = pl.pallas_call(
             functools.partial(later_kernel, shifts),
             in_specs=[SMEM] + [VMEM] * 5 + [pl.BlockSpec(memory_space=pl.ANY)] * len(arrived),

time: 85.8 us -> 84.3 us (0.983); the launches traced: 84.3 us -> 84.4 us
  blocking collectives: 0 us -> 36.9 us
  waiting for transfers between devices: 28.5 us -> 3.25 us
  starting transfers between devices: 23.7 us -> 14.5 us
  other arithmetic: 4.48 us -> 1.68 us
  Pallas kernels: 26.2 us -> 27.8 us
  local copies, waits for them, and re-layouts: 1.28 us -> 0.04 us
    all_to_all x0 -> x1, blocking collectives: none -> 36.9 us  [local(): lax.all_to_all(packed, DEVICES, split_axis=0, concat_axis=0, tiled=True)]
    all_to_all x1 -> x0, waiting for transfers between devices: 25.2 us -> none  [local(): lax.all_to_all(packed, DEVICES, split_axis=0, concat_axis=0, tiled=True)]
    all_to_all x1 -> x0, starting transfers between devices: 8.74 us -> none  [local(): lax.all_to_all(packed, DEVICES, split_axis=0, concat_axis=0, tiled=True)]
    pallas_call x2 -> x3, Pallas kernels: 14.8 us -> 18.8 us  [local(): pl.pallas_call(functools.partial(later_kernel, shifts), in_specs=[SMEM] +...]
    pallas_call x1, Pallas kernels: 9.86 us -> 7.46 us  [local(): pl.pallas_call(functools.partial(first_kernel, GROUPS[0]), in_specs=[SMEM...]
    concatenate x1, other arithmetic: 3.1 us -> 1.68 us  [local(): packed = jnp.concatenate([prefix_keys[0], prefix_values[0]], axis=1)]
    another operation x1 -> x0, other arithmetic: 1.38 us -> none  [local(): place = jnp.stack([request, me, hit_len[request], suffix_len[request]])]
    dynamic_slice x2 -> x0, local copies, waits for them, and re-layouts: 1.26 us -> none  [local(): place = jnp.stack([request, me, hit_len[request], suffix_len[request]])]
  transfers between devices with their start and end apart: 8 -> 7, of which waited for: 3 -> 2; matrix products, arithmetic and copies ran while one was open for 3% -> 0% of each run, Pallas kernels for 18% -> 22%
where the time goes in v3:
time: 84.3 us; the launch traced here: 84.4 us
  blocking collectives  36.9 us (44%)
  Pallas kernels  27.8 us (33%)
  starting transfers between devices  14.5 us (17%)
  waiting for transfers between devices  3.25 us (4%)
  other arithmetic  1.68 us (2%)
    all_to_all x1, blocking collectives, local(): lax.all_to_all(packed, DEVICES, split_axis=0, concat_axis=0, tiled=True)  36.9 us
    pallas_call x3, Pallas kernels, local(): pl.pallas_call(functools.partial(later_kernel, shifts), in_specs=[SMEM] +...  18.8 us
    ppermute x7, starting transfers between devices, send(): lax.ppermute(x, 'tensor', [(z, (z + d) % 8) for z in range(8)])  14.5 us
    pallas_call x1, Pallas kernels, local(): pl.pallas_call(functools.partial(first_kernel, GROUPS[0]), in_specs=[SMEM...  7.46 us
    ppermute x7, waiting for transfers between devices, send(): lax.ppermute(x, 'tensor', [(z, (z + d) % 8) for z in range(8)])  3.25 us
  transfers between devices with their start and end apart: 7, of which 2 were waited for; matrix products, arithmetic and copies ran while one was open for 0% of the time, Pallas kernels for 22%

profile of v3, /device:TPU:1, one launch (start us, length us, event | category | flops | bytes accessed | tf_op | source)
XLA Modules:
  0.0 84.4 jit_solution(13712518824085497716)
XLA Ops:
  0.0 1.7 %pad_maximum_fusion = bf16[32,256,128]{2,1,0:T(8,128)(2,1)S(1)} fusion(bf16[32,128,128]{2,1,0:T(8,128)(2,1)} %bitcast.17, bf16[32,128,128]{2,1,0:T(8,128)(2,1)} %bitcast.18), kind=kLoop, calls=%fused_computation | loop fusion | flops 4194304 | bytes 4194304 | tf_op jit(solution)/shard_map/concatenate | solution.py:150
  1.7 0.0 copy-start
  1.7 0.0 copy-start.1
  1.7 0.0 copy-start.2
  1.7 0.0 copy-start.3
  1.7 0.0 copy-start.4
  1.7 0.0 copy-start.5
  1.8 36.9 %all_to_all.5.buf_ref = bf16[32,256,128]{2,1,0:T(8,128)(2,1)S(1)} all-to-all(bf16[32,256,128]{2,1,0:T(8,128)(2,1)S(1)} %pad_maximum_fusion), channel_id=1, replica_groups=mesh['dp'=4,'cache'=8,'tensor'=8] {'dp','cache'}, dimensions={0} | all-to-all | bytes 4194304 | tf_op jit(solution)/shard_map/all_to_all | solution.py:151
  38.7 0.0 copy-done
  38.7 0.0 copy-done.1
  38.7 0.0 copy-done.2
  38.7 0.0 copy-done.3
  38.7 0.0 copy-done.4
  38.7 0.0 copy-done.5
  38.7 7.5 %attend_first.1 = (s32[4]{0:T(128)S(1)}, bf16[4096,128]{1,0:T(8,128)(2,1)S(1)}, bf16[4096,256]{1,0:T(8,128)(2,1)S(1)}, bf16[32,2048]{1,0:T(8,128)(2,1)S(1)}, bf16[32,2048]{1,0:T(8,128)(2,1)S(1)}) custom-call(s32[32]{0:T(128)S(1)} %copy-done.4, s32[32]{0:T(128)S(1)} %copy-done.5, s32[32,32]{1,0:T(8,128)S(1)} %copy-done.3, bf16[8,32,2048]{2,1,0:T(8,128)(2,1)S(1)} %bitcast.5, ...), custom_call_target="tpu_custom_call" | custom-call | tf_op jit(solution)/shard_map/attend_first/pallas_call | solution.py:154
  46.2 7.0 %collective-permute-start = (bf16[32,2048]{1,0:T(8,128)(2,1)S(1)}, bf16[32,2048]{1,0:T(8,128)(2,1)S(1)}, u32[]{:S(2)}, u32[]{:S(2)}) collective-permute-start(bf16[32,2048]{1,0:T(8,128)(2,1)S(1)} %get-tuple-element.16), channel_id=1, source_target_pairs={{0,4},{1,5},{2,6},{3,7},{4,0},{5,1},{6,2},{7,3},{8,12},{9,13},{10,... | collective-permute-start | bytes 393224 | tf_op jit(solution)/shard_map/ppermute | solution.py:164
  53.2 0.0 collective-permute-start.1
  53.2 9.1 %attend_later.3 = (bf16[32,2048]{1,0:T(8,128)(2,1)S(1)}, bf16[32,2048]{1,0:T(8,128)(2,1)S(1)}, bf16[32,2048]{1,0:T(8,128)(2,1)S(1)}) custom-call(s32[4]{0:T(128)S(1)} %get-tuple-element.15.place, bf16[8,32,2048]{2,1,0:T(8,128)(2,1)S(1)} %bitcast.6, bf16[256,128]{1,0:T(8,128)(2,1)S(1)} %bitcast.10, bf16[256,128]{1,0:T(8,128)(2,1)S(1)} %bitcast.14, ...), custom_call_target="tpu_custom_call" | custom-call | tf_op jit(solution)/shard_map/attend_later/pallas_call | solution.py:173
  62.2 3.3 %collective-permute-start.2 = (bf16[32,2048]{1,0:T(8,128)(2,1)S(1)}, bf16[32,2048]{1,0:T(8,128)(2,1)S(1)}, u32[]{:S(2)}, u32[]{:S(2)}) collective-permute-start(bf16[32,2048]{1,0:T(8,128)(2,1)S(1)} %get-tuple-element.20), channel_id=1, source_target_pairs={{0,3},{1,4},{2,5},{3,6},{4,7},{5,0},{6,1},{7,2},{8,11},{9,12},{10,... | collective-permute-start | bytes 393224 | tf_op jit(solution)/shard_map/ppermute | solution.py:164
  65.6 0.9 %collective-permute-start.3 = (bf16[32,2048]{1,0:T(8,128)(2,1)S(1)}, bf16[32,2048]{1,0:T(8,128)(2,1)S(1)}, u32[]{:S(2)}, u32[]{:S(2)}) collective-permute-start(bf16[32,2048]{1,0:T(8,128)(2,1)S(1)} %get-tuple-element.21), channel_id=1, source_target_pairs={{0,6},{1,7},{2,0},{3,1},{4,2},{5,3},{6,4},{7,5},{8,14},{9,15},{10,... | collective-permute-start | bytes 393224 | tf_op jit(solution)/shard_map/ppermute | solution.py:164
  66.5 1.5 %collective-permute-start.4 = (bf16[32,2048]{1,0:T(8,128)(2,1)S(1)}, bf16[32,2048]{1,0:T(8,128)(2,1)S(1)}, u32[]{:S(2)}, u32[]{:S(2)}) collective-permute-start(bf16[32,2048]{1,0:T(8,128)(2,1)S(1)} %get-tuple-element.22), channel_id=1, source_target_pairs={{0,2},{1,3},{2,4},{3,5},{4,6},{5,7},{6,0},{7,1},{8,10},{9,11},{10,... | collective-permute-start | bytes 393224 | tf_op jit(solution)/shard_map/ppermute | solution.py:164
  68.0 0.0 collective-permute-done.refs_0_
  68.0 0.9 %collective-permute-done.1.refs_1_ = bf16[32,2048]{1,0:T(8,128)(2,1)S(1)} collective-permute-done((bf16[32,2048]{1,0:T(8,128)(2,1)S(1)}, bf16[32,2048]{1,0:T(8,128)(2,1)S(1)}, u32[]{:S(2)}, u32[]{:S(2)}) %collective-permute-start.1) | collective-permute-done | bytes 131104 | tf_op jit(solution)/shard_map/ppermute | solution.py:164
  68.8 6.3 %attend_later.4 = (bf16[32,2048]{1,0:T(8,128)(2,1)S(1)}, bf16[32,2048]{1,0:T(8,128)(2,1)S(1)}) custom-call(s32[4]{0:T(128)S(1)} %get-tuple-element.15.place, bf16[8,32,2048]{2,1,0:T(8,128)(2,1)S(1)} %bitcast.7, bf16[256,128]{1,0:T(8,128)(2,1)S(1)} %bitcast.11, bf16[256,128]{1,0:T(8,128)(2,1)S(1)} %bitcast.15, bf16[4096,128]{1,0:T(8,128)(2,1)S(1)} %get-tuple-element.18.k_ref, ...), custom_call_target="tpu_custom_call" | custom-call | tf_op jit(solution)/shard_map/attend_later/pallas_call | solution.py:173
  75.1 1.8 %collective-permute-start.5 = (bf16[32,2048]{1,0:T(8,128)(2,1)S(1)}, bf16[32,2048]{1,0:T(8,128)(2,1)S(1)}, u32[]{:S(2)}, u32[]{:S(2)}) collective-permute-start(bf16[32,2048]{1,0:T(8,128)(2,1)S(1)} %get-tuple-element.23), channel_id=1, source_target_pairs={{0,7},{1,0},{2,1},{3,2},{4,3},{5,4},{6,5},{7,6},{8,15},{9,8},{10,9... | collective-permute-start | bytes 393224 | tf_op jit(solution)/shard_map/ppermute | solution.py:164
  76.9 0.0 collective-permute-start.6
  76.9 0.0 collective-permute-done.2.refs_0_.refs_2_
  76.9 3.4 %attend_later.5.refs_7_ = bf16[32,2048]{1,0:T(8,128)(2,1)S(1)} custom-call(s32[4]{0:T(128)S(1)} %get-tuple-element.15.place, bf16[8,32,2048]{2,1,0:T(8,128)(2,1)S(1)} %bitcast.8, bf16[256,128]{1,0:T(8,128)(2,1)S(1)} %bitcast.12, bf16[256,128]{1,0:T(8,128)(2,1)S(1)} %bitcast.16, bf16[4096,128]{1,0:T(8,128)(2,1)S(1)} %get-tuple-element.18.k_ref, ...), custom_call_target="tpu_custom_call" | custom-call | tf_op jit(solution)/shard_map/attend_later/pallas_call | solution.py:173
  80.4 0.0 collective-permute-done.3.refs_3_
  80.4 0.0 collective-permute-done.4.refs_4_
  80.4 0.0 collective-permute-done.5.refs_5_
  80.4 2.4 %collective-permute-done.6.refs_6_ = bf16[32,2048]{1,0:T(8,128)(2,1)S(1)} collective-permute-done((bf16[32,2048]{1,0:T(8,128)(2,1)S(1)}, bf16[32,2048]{1,0:T(8,128)(2,1)S(1)}, u32[]{:S(2)}, u32[]{:S(2)}) %collective-permute-start.6) | collective-permute-done | bytes 131104 | tf_op jit(solution)/shard_map/ppermute | solution.py:164
  82.8 1.6 %gather_blocks.1 = bf16[1,32,16384]{2,1,0:T(8,128)(2,1)} custom-call(s32[4]{0:T(128)S(1)} %get-tuple-element.15.place, bf16[32,2048]{1,0:T(8,128)(2,1)S(1)} %collective-permute-done.refs_0_, bf16[32,2048]{1,0:T(8,128)(2,1)S(1)} %collective-permute-done.1.refs_1_, bf16[32,2048]{1,0:T(8,128)(2,1)S(1)} %collective-permute-done.2.refs_0_.refs_2_, ...), custom_call_target="tpu_custom_call" | custom-call | tf_op jit(solution)/shard_map/gather_blocks/pallas_call | solution.py:183
Async XLA Ops:
  1.7 37.0 %copy-start = (bf16[1,256,2048]{2,1,0:T(8,128)(2,1)S(1)}, bf16[1,256,2048]{2,1,0:T(8,128)(2,1)}, u32[]{:S(2)}) copy-start(bf16[1,256,2048]{2,1,0:T(8,128)(2,1)} %param.8) | copy-start | bytes 3145732
  1.7 37.0 %copy-start.1 = (bf16[1,256,128]{2,1,0:T(8,128)(2,1)S(1)}, bf16[1,256,128]{2,1,0:T(8,128)(2,1)}, u32[]{:S(2)}) copy-start(bf16[1,256,128]{2,1,0:T(8,128)(2,1)} %param.9) | copy-start | bytes 196612
  1.7 37.0 %copy-start.2 = (bf16[1,256,128]{2,1,0:T(8,128)(2,1)S(1)}, bf16[1,256,128]{2,1,0:T(8,128)(2,1)}, u32[]{:S(2)}) copy-start(bf16[1,256,128]{2,1,0:T(8,128)(2,1)} %param.10) | copy-start | bytes 196612
  1.7 37.0 %copy-start.3 = (s32[32,32]{1,0:T(8,128)S(1)}, s32[32,32]{1,0:T(8,128)}, u32[]{:S(2)}) copy-start(s32[32,32]{1,0:T(8,128)} %page_map.1) | copy-start | bytes 12292
  1.7 37.0 %copy-start.4 = (s32[32]{0:T(128)S(1)}, s32[32]{0:T(128)}, u32[]{:S(2)}) copy-start(s32[32]{0:T(128)} %hit_len.1) | copy-start | bytes 388
  1.7 37.0 %copy-start.5 = (s32[32]{0:T(128)S(1)}, s32[32]{0:T(128)}, u32[]{:S(2)}) copy-start(s32[32]{0:T(128)} %suffix_len.1) | copy-start | bytes 388
  46.2 21.8 %collective-permute-start = (bf16[32,2048]{1,0:T(8,128)(2,1)S(1)}, bf16[32,2048]{1,0:T(8,128)(2,1)S(1)}, u32[]{:S(2)}, u32[]{:S(2)}) collective-permute-start(bf16[32,2048]{1,0:T(8,128)(2,1)S(1)} %get-tuple-element.16), channel_id=1, source_target_pairs={{0,4},{1,5},{2,6},{3,7},{4,0},{5,1},{6,2},{7,3},{8,12},{9,13},{10,... | collective-permute-start | bytes 393224 | tf_op jit(solution)/shard_map/ppermute | solution.py:164
  53.2 15.7 %collective-permute-start.1 = (bf16[32,2048]{1,0:T(8,128)(2,1)S(1)}, bf16[32,2048]{1,0:T(8,128)(2,1)S(1)}, u32[]{:S(2)}, u32[]{:S(2)}) collective-permute-start(bf16[32,2048]{1,0:T(8,128)(2,1)S(1)} %get-tuple-element.17), channel_id=1, source_target_pairs={{0,5},{1,6},{2,7},{3,0},{4,1},{5,2},{6,3},{7,4},{8,13},{9,14},{10,... | collective-permute-start | bytes 393224 | tf_op jit(solution)/shard_map/ppermute | solution.py:164
  62.2 14.7 %collective-permute-start.2 = (bf16[32,2048]{1,0:T(8,128)(2,1)S(1)}, bf16[32,2048]{1,0:T(8,128)(2,1)S(1)}, u32[]{:S(2)}, u32[]{:S(2)}) collective-permute-start(bf16[32,2048]{1,0:T(8,128)(2,1)S(1)} %get-tuple-element.20), channel_id=1, source_target_pairs={{0,3},{1,4},{2,5},{3,6},{4,7},{5,0},{6,1},{7,2},{8,11},{9,12},{10,... | collective-permute-start | bytes 393224 | tf_op jit(solution)/shard_map/ppermute | solution.py:164
  65.6 14.8 %collective-permute-start.3 = (bf16[32,2048]{1,0:T(8,128)(2,1)S(1)}, bf16[32,2048]{1,0:T(8,128)(2,1)S(1)}, u32[]{:S(2)}, u32[]{:S(2)}) collective-permute-start(bf16[32,2048]{1,0:T(8,128)(2,1)S(1)} %get-tuple-element.21), channel_id=1, source_target_pairs={{0,6},{1,7},{2,0},{3,1},{4,2},{5,3},{6,4},{7,5},{8,14},{9,15},{10,... | collective-permute-start | bytes 393224 | tf_op jit(solution)/shard_map/ppermute | solution.py:164
  66.5 13.9 %collective-permute-start.4 = (bf16[32,2048]{1,0:T(8,128)(2,1)S(1)}, bf16[32,2048]{1,0:T(8,128)(2,1)S(1)}, u32[]{:S(2)}, u32[]{:S(2)}) collective-permute-start(bf16[32,2048]{1,0:T(8,128)(2,1)S(1)} %get-tuple-element.22), channel_id=1, source_target_pairs={{0,2},{1,3},{2,4},{3,5},{4,6},{5,7},{6,0},{7,1},{8,10},{9,11},{10,... | collective-permute-start | bytes 393224 | tf_op jit(solution)/shard_map/ppermute | solution.py:164
  75.1 5.3 %collective-permute-start.5 = (bf16[32,2048]{1,0:T(8,128)(2,1)S(1)}, bf16[32,2048]{1,0:T(8,128)(2,1)S(1)}, u32[]{:S(2)}, u32[]{:S(2)}) collective-permute-start(bf16[32,2048]{1,0:T(8,128)(2,1)S(1)} %get-tuple-element.23), channel_id=1, source_target_pairs={{0,7},{1,0},{2,1},{3,2},{4,3},{5,4},{6,5},{7,6},{8,15},{9,8},{10,9... | collective-permute-start | bytes 393224 | tf_op jit(solution)/shard_map/ppermute | solution.py:164
  76.9 5.9 %collective-permute-start.6 = (bf16[32,2048]{1,0:T(8,128)(2,1)S(1)}, bf16[32,2048]{1,0:T(8,128)(2,1)S(1)}, u32[]{:S(2)}, u32[]{:S(2)}) collective-permute-start(bf16[32,2048]{1,0:T(8,128)(2,1)S(1)} %get-tuple-element.24), channel_id=1, source_target_pairs={{0,1},{1,2},{2,3},{3,4},{4,5},{5,6},{6,7},{7,0},{8,9},{9,10},{10,1... | collective-permute-start | bytes 393224 | tf_op jit(solution)/shard_map/ppermute | solution.py:164

commit v4 on v3

--- a/solution.py
+++ b/solution.py
@@ -19,7 +19,7 @@
 RB = ROWS * HEADS
 TILE = 1024
 RS = 512
-GROUPS = ((4, 5), (3, 6, 2), (7, 1), (0,))
+GROUPS = ((3, 5), (4, 6, 2), (7, 1), (0,))
 SCALE = math.log2(math.e) / math.sqrt(HD)
 F32 = jnp.float32
 BF16 = jnp.bfloat16

time: 84.3 us -> 83.7 us (level)
  waiting for transfers between devices: 3.25 us -> 1.82 us
  starting transfers between devices: 14.5 us -> 15.5 us
    ppermute x7, waiting for transfers between devices: 3.25 us -> 1.82 us  [send(): lax.ppermute(x, 'tensor', [(z, (z + d) % 8) for z in range(8)])]
    ppermute x7, starting transfers between devices: 14.5 us -> 15.5 us  [send(): lax.ppermute(x, 'tensor', [(z, (z + d) % 8) for z in range(8)])]
  transfers between devices with their start and end apart: 7 -> 7, of which waited for: 2 -> 1; matrix products, arithmetic and copies ran while one was open for 0% -> 0% of each run, Pallas kernels for 22% -> 22%
where the time goes in v4:
time: 83.7 us; the launch traced here: 83.9 us
  blocking collectives  36.9 us (44%)
  Pallas kernels  27.8 us (33%)
  starting transfers between devices  15.5 us (19%)
  waiting for transfers between devices  1.82 us (2%)
  other arithmetic  1.68 us (2%)
    all_to_all x1, blocking collectives, local(): lax.all_to_all(packed, DEVICES, split_axis=0, concat_axis=0, tiled=True)  36.9 us
    pallas_call x3, Pallas kernels, local(): pl.pallas_call(functools.partial(later_kernel, shifts), in_specs=[SMEM] +...  18.8 us
    ppermute x7, starting transfers between devices, send(): lax.ppermute(x, 'tensor', [(z, (z + d) % 8) for z in range(8)])  15.5 us
    pallas_call x1, Pallas kernels, local(): pl.pallas_call(functools.partial(first_kernel, GROUPS[0]), in_specs=[SMEM...  7.46 us
    ppermute x7, waiting for transfers between devices, send(): lax.ppermute(x, 'tensor', [(z, (z + d) % 8) for z in range(8)])  1.82 us
    concatenate x1, other arithmetic, local(): packed = jnp.concatenate([prefix_keys[0], prefix_values[0]], axis=1)  1.68 us
  transfers between devices with their start and end apart: 7, of which 1 were waited for; matrix products, arithmetic and copies ran while one was open for 0% of the time, Pallas kernels for 22%

profile of v4, /device:TPU:1, one launch (start us, length us, event | category | flops | bytes accessed | tf_op | source)
XLA Modules:
  0.0 83.9 jit_solution(7687624518873214234)
XLA Ops:
  0.0 1.7 %pad_maximum_fusion = bf16[32,256,128]{2,1,0:T(8,128)(2,1)S(1)} fusion(bf16[32,128,128]{2,1,0:T(8,128)(2,1)} %bitcast.17, bf16[32,128,128]{2,1,0:T(8,128)(2,1)} %bitcast.18), kind=kLoop, calls=%fused_computation | loop fusion | flops 4194304 | bytes 4194304 | tf_op jit(solution)/shard_map/concatenate | solution.py:150
  1.7 0.0 copy-start
  1.7 0.0 copy-start.1
  1.7 0.0 copy-start.2
  1.7 0.0 copy-start.3
  1.7 0.0 copy-start.4
  1.7 0.0 copy-start.5
  1.8 36.9 %all_to_all.5.buf_ref = bf16[32,256,128]{2,1,0:T(8,128)(2,1)S(1)} all-to-all(bf16[32,256,128]{2,1,0:T(8,128)(2,1)S(1)} %pad_maximum_fusion), channel_id=1, replica_groups=mesh['dp'=4,'cache'=8,'tensor'=8] {'dp','cache'}, dimensions={0} | all-to-all | bytes 4194304 | tf_op jit(solution)/shard_map/all_to_all | solution.py:151
  38.7 0.0 copy-done
  38.7 0.0 copy-done.1
  38.7 0.0 copy-done.2
  38.7 0.0 copy-done.3
  38.7 0.0 copy-done.4
  38.7 0.0 copy-done.5
  38.7 7.5 %attend_first.1 = (s32[4]{0:T(128)S(1)}, bf16[4096,128]{1,0:T(8,128)(2,1)S(1)}, bf16[4096,256]{1,0:T(8,128)(2,1)S(1)}, bf16[32,2048]{1,0:T(8,128)(2,1)S(1)}, bf16[32,2048]{1,0:T(8,128)(2,1)S(1)}) custom-call(s32[32]{0:T(128)S(1)} %copy-done.4, s32[32]{0:T(128)S(1)} %copy-done.5, s32[32,32]{1,0:T(8,128)S(1)} %copy-done.3, bf16[8,32,2048]{2,1,0:T(8,128)(2,1)S(1)} %bitcast.5, ...), custom_call_target="tpu_custom_call" | custom-call | tf_op jit(solution)/shard_map/attend_first/pallas_call | solution.py:154
  46.2 4.4 %collective-permute-start = (bf16[32,2048]{1,0:T(8,128)(2,1)S(1)}, bf16[32,2048]{1,0:T(8,128)(2,1)S(1)}, u32[]{:S(2)}, u32[]{:S(2)}) collective-permute-start(bf16[32,2048]{1,0:T(8,128)(2,1)S(1)} %get-tuple-element.16), channel_id=1, source_target_pairs={{0,3},{1,4},{2,5},{3,6},{4,7},{5,0},{6,1},{7,2},{8,11},{9,12},{10,... | collective-permute-start | bytes 393224 | tf_op jit(solution)/shard_map/ppermute | solution.py:164
  50.6 2.4 %collective-permute-start.1 = (bf16[32,2048]{1,0:T(8,128)(2,1)S(1)}, bf16[32,2048]{1,0:T(8,128)(2,1)S(1)}, u32[]{:S(2)}, u32[]{:S(2)}) collective-permute-start(bf16[32,2048]{1,0:T(8,128)(2,1)S(1)} %get-tuple-element.17), channel_id=1, source_target_pairs={{0,5},{1,6},{2,7},{3,0},{4,1},{5,2},{6,3},{7,4},{8,13},{9,14},{10,... | collective-permute-start | bytes 393224 | tf_op jit(solution)/shard_map/ppermute | solution.py:164
  53.0 9.1 %attend_later.3 = (bf16[32,2048]{1,0:T(8,128)(2,1)S(1)}, bf16[32,2048]{1,0:T(8,128)(2,1)S(1)}, bf16[32,2048]{1,0:T(8,128)(2,1)S(1)}) custom-call(s32[4]{0:T(128)S(1)} %get-tuple-element.15.place, bf16[8,32,2048]{2,1,0:T(8,128)(2,1)S(1)} %bitcast.6, bf16[256,128]{1,0:T(8,128)(2,1)S(1)} %bitcast.10, bf16[256,128]{1,0:T(8,128)(2,1)S(1)} %bitcast.14, ...), custom_call_target="tpu_custom_call" | custom-call | tf_op jit(solution)/shard_map/attend_later/pallas_call | solution.py:173
  62.1 4.7 %collective-permute-start.2 = (bf16[32,2048]{1,0:T(8,128)(2,1)S(1)}, bf16[32,2048]{1,0:T(8,128)(2,1)S(1)}, u32[]{:S(2)}, u32[]{:S(2)}) collective-permute-start(bf16[32,2048]{1,0:T(8,128)(2,1)S(1)} %get-tuple-element.20), channel_id=1, source_target_pairs={{0,4},{1,5},{2,6},{3,7},{4,0},{5,1},{6,2},{7,3},{8,12},{9,13},{10,... | collective-permute-start | bytes 393224 | tf_op jit(solution)/shard_map/ppermute | solution.py:164
  66.8 0.0 collective-permute-start.3
  66.8 2.4 %collective-permute-start.4 = (bf16[32,2048]{1,0:T(8,128)(2,1)S(1)}, bf16[32,2048]{1,0:T(8,128)(2,1)S(1)}, u32[]{:S(2)}, u32[]{:S(2)}) collective-permute-start(bf16[32,2048]{1,0:T(8,128)(2,1)S(1)} %get-tuple-element.22), channel_id=1, source_target_pairs={{0,2},{1,3},{2,4},{3,5},{4,6},{5,7},{6,0},{7,1},{8,10},{9,11},{10,... | collective-permute-start | bytes 393224 | tf_op jit(solution)/shard_map/ppermute | solution.py:164
  69.2 0.0 collective-permute-done.refs_0_
  69.2 0.0 collective-permute-done.1.refs_1_
  69.2 6.3 %attend_later.4 = (bf16[32,2048]{1,0:T(8,128)(2,1)S(1)}, bf16[32,2048]{1,0:T(8,128)(2,1)S(1)}) custom-call(s32[4]{0:T(128)S(1)} %get-tuple-element.15.place, bf16[8,32,2048]{2,1,0:T(8,128)(2,1)S(1)} %bitcast.7, bf16[256,128]{1,0:T(8,128)(2,1)S(1)} %bitcast.11, bf16[256,128]{1,0:T(8,128)(2,1)S(1)} %bitcast.15, bf16[4096,128]{1,0:T(8,128)(2,1)S(1)} %get-tuple-element.18.k_ref, ...), custom_call_target="tpu_custom_call" | custom-call | tf_op jit(solution)/shard_map/attend_later/pallas_call | solution.py:173
  75.4 0.8 %collective-permute-start.5 = (bf16[32,2048]{1,0:T(8,128)(2,1)S(1)}, bf16[32,2048]{1,0:T(8,128)(2,1)S(1)}, u32[]{:S(2)}, u32[]{:S(2)}) collective-permute-start(bf16[32,2048]{1,0:T(8,128)(2,1)S(1)} %get-tuple-element.23), channel_id=1, source_target_pairs={{0,7},{1,0},{2,1},{3,2},{4,3},{5,4},{6,5},{7,6},{8,15},{9,8},{10,9... | collective-permute-start | bytes 393224 | tf_op jit(solution)/shard_map/ppermute | solution.py:164
  76.3 0.7 collective-permute-start.6
  77.0 0.0 collective-permute-done.2.refs_0_.refs_2_
  77.0 3.4 %attend_later.5.refs_7_ = bf16[32,2048]{1,0:T(8,128)(2,1)S(1)} custom-call(s32[4]{0:T(128)S(1)} %get-tuple-element.15.place, bf16[8,32,2048]{2,1,0:T(8,128)(2,1)S(1)} %bitcast.8, bf16[256,128]{1,0:T(8,128)(2,1)S(1)} %bitcast.12, bf16[256,128]{1,0:T(8,128)(2,1)S(1)} %bitcast.16, bf16[4096,128]{1,0:T(8,128)(2,1)S(1)} %get-tuple-element.18.k_ref, ...), custom_call_target="tpu_custom_call" | custom-call | tf_op jit(solution)/shard_map/attend_later/pallas_call | solution.py:173
  80.4 0.0 collective-permute-done.3.refs_3_
  80.4 0.0 collective-permute-done.4.refs_4_
  80.5 1.8 %collective-permute-done.5.refs_5_ = bf16[32,2048]{1,0:T(8,128)(2,1)S(1)} collective-permute-done((bf16[32,2048]{1,0:T(8,128)(2,1)S(1)}, bf16[32,2048]{1,0:T(8,128)(2,1)S(1)}, u32[]{:S(2)}, u32[]{:S(2)}) %collective-permute-start.5) | collective-permute-done | bytes 131104 | tf_op jit(solution)/shard_map/ppermute | solution.py:164
  82.3 0.0 collective-permute-done.6.refs_6_
  82.3 1.6 %gather_blocks.1 = bf16[1,32,16384]{2,1,0:T(8,128)(2,1)} custom-call(s32[4]{0:T(128)S(1)} %get-tuple-element.15.place, bf16[32,2048]{1,0:T(8,128)(2,1)S(1)} %collective-permute-done.refs_0_, bf16[32,2048]{1,0:T(8,128)(2,1)S(1)} %collective-permute-done.1.refs_1_, bf16[32,2048]{1,0:T(8,128)(2,1)S(1)} %collective-permute-done.2.refs_0_.refs_2_, ...), custom_call_target="tpu_custom_call" | custom-call | tf_op jit(solution)/shard_map/gather_blocks/pallas_call | solution.py:183
Async XLA Ops:
  1.7 37.0 %copy-start = (bf16[1,256,2048]{2,1,0:T(8,128)(2,1)S(1)}, bf16[1,256,2048]{2,1,0:T(8,128)(2,1)}, u32[]{:S(2)}) copy-start(bf16[1,256,2048]{2,1,0:T(8,128)(2,1)} %param.8) | copy-start | bytes 3145732
  1.7 37.0 %copy-start.1 = (bf16[1,256,128]{2,1,0:T(8,128)(2,1)S(1)}, bf16[1,256,128]{2,1,0:T(8,128)(2,1)}, u32[]{:S(2)}) copy-start(bf16[1,256,128]{2,1,0:T(8,128)(2,1)} %param.9) | copy-start | bytes 196612
  1.7 37.0 %copy-start.2 = (bf16[1,256,128]{2,1,0:T(8,128)(2,1)S(1)}, bf16[1,256,128]{2,1,0:T(8,128)(2,1)}, u32[]{:S(2)}) copy-start(bf16[1,256,128]{2,1,0:T(8,128)(2,1)} %param.10) | copy-start | bytes 196612
  1.7 37.0 %copy-start.3 = (s32[32,32]{1,0:T(8,128)S(1)}, s32[32,32]{1,0:T(8,128)}, u32[]{:S(2)}) copy-start(s32[32,32]{1,0:T(8,128)} %page_map.1) | copy-start | bytes 12292
  1.7 37.0 %copy-start.4 = (s32[32]{0:T(128)S(1)}, s32[32]{0:T(128)}, u32[]{:S(2)}) copy-start(s32[32]{0:T(128)} %hit_len.1) | copy-start | bytes 388
  1.7 37.0 %copy-start.5 = (s32[32]{0:T(128)S(1)}, s32[32]{0:T(128)}, u32[]{:S(2)}) copy-start(s32[32]{0:T(128)} %suffix_len.1) | copy-start | bytes 388
  46.2 23.0 %collective-permute-start = (bf16[32,2048]{1,0:T(8,128)(2,1)S(1)}, bf16[32,2048]{1,0:T(8,128)(2,1)S(1)}, u32[]{:S(2)}, u32[]{:S(2)}) collective-permute-start(bf16[32,2048]{1,0:T(8,128)(2,1)S(1)} %get-tuple-element.16), channel_id=1, source_target_pairs={{0,3},{1,4},{2,5},{3,6},{4,7},{5,0},{6,1},{7,2},{8,11},{9,12},{10,... | collective-permute-start | bytes 393224 | tf_op jit(solution)/shard_map/ppermute | solution.py:164
  50.6 18.6 %collective-permute-start.1 = (bf16[32,2048]{1,0:T(8,128)(2,1)S(1)}, bf16[32,2048]{1,0:T(8,128)(2,1)S(1)}, u32[]{:S(2)}, u32[]{:S(2)}) collective-permute-start(bf16[32,2048]{1,0:T(8,128)(2,1)S(1)} %get-tuple-element.17), channel_id=1, source_target_pairs={{0,5},{1,6},{2,7},{3,0},{4,1},{5,2},{6,3},{7,4},{8,13},{9,14},{10,... | collective-permute-start | bytes 393224 | tf_op jit(solution)/shard_map/ppermute | solution.py:164
  62.1 14.9 %collective-permute-start.2 = (bf16[32,2048]{1,0:T(8,128)(2,1)S(1)}, bf16[32,2048]{1,0:T(8,128)(2,1)S(1)}, u32[]{:S(2)}, u32[]{:S(2)}) collective-permute-start(bf16[32,2048]{1,0:T(8,128)(2,1)S(1)} %get-tuple-element.20), channel_id=1, source_target_pairs={{0,4},{1,5},{2,6},{3,7},{4,0},{5,1},{6,2},{7,3},{8,12},{9,13},{10,... | collective-permute-start | bytes 393224 | tf_op jit(solution)/shard_map/ppermute | solution.py:164
  66.8 13.6 %collective-permute-start.3 = (bf16[32,2048]{1,0:T(8,128)(2,1)S(1)}, bf16[32,2048]{1,0:T(8,128)(2,1)S(1)}, u32[]{:S(2)}, u32[]{:S(2)}) collective-permute-start(bf16[32,2048]{1,0:T(8,128)(2,1)S(1)} %get-tuple-element.21), channel_id=1, source_target_pairs={{0,6},{1,7},{2,0},{3,1},{4,2},{5,3},{6,4},{7,5},{8,14},{9,15},{10,... | collective-permute-start | bytes 393224 | tf_op jit(solution)/shard_map/ppermute | solution.py:164
  66.8 13.6 %collective-permute-start.4 = (bf16[32,2048]{1,0:T(8,128)(2,1)S(1)}, bf16[32,2048]{1,0:T(8,128)(2,1)S(1)}, u32[]{:S(2)}, u32[]{:S(2)}) collective-permute-start(bf16[32,2048]{1,0:T(8,128)(2,1)S(1)} %get-tuple-element.22), channel_id=1, source_target_pairs={{0,2},{1,3},{2,4},{3,5},{4,6},{5,7},{6,0},{7,1},{8,10},{9,11},{10,... | collective-permute-start | bytes 393224 | tf_op jit(solution)/shard_map/ppermute | solution.py:164
  75.4 6.8 %collective-permute-start.5 = (bf16[32,2048]{1,0:T(8,128)(2,1)S(1)}, bf16[32,2048]{1,0:T(8,128)(2,1)S(1)}, u32[]{:S(2)}, u32[]{:S(2)}) collective-permute-start(bf16[32,2048]{1,0:T(8,128)(2,1)S(1)} %get-tuple-element.23), channel_id=1, source_target_pairs={{0,7},{1,0},{2,1},{3,2},{4,3},{5,4},{6,5},{7,6},{8,15},{9,8},{10,9... | collective-permute-start | bytes 393224 | tf_op jit(solution)/shard_map/ppermute | solution.py:164
  76.3 6.0 %collective-permute-start.6 = (bf16[32,2048]{1,0:T(8,128)(2,1)S(1)}, bf16[32,2048]{1,0:T(8,128)(2,1)S(1)}, u32[]{:S(2)}, u32[]{:S(2)}) collective-permute-start(bf16[32,2048]{1,0:T(8,128)(2,1)S(1)} %get-tuple-element.24), channel_id=1, source_target_pairs={{0,1},{1,2},{2,3},{3,4},{4,5},{5,6},{6,7},{7,0},{8,9},{9,10},{10,1... | collective-permute-start | bytes 393224 | tf_op jit(solution)/shard_map/ppermute | solution.py:164

commit v5 on v4

--- a/solution.py
+++ b/solution.py
@@ -139,9 +139,10 @@
 
 def gather_kernel(place, *refs):
     out_ref = refs[-1]
+    rows = pl.ds(pl.multiple_of(pl.program_id(0) * (ROWS // 2), ROWS // 2), ROWS // 2)
     for block, shift in zip(refs, sum(GROUPS, ())):
         source = lax.rem(place[1] + 8 - shift, 8)
-        out_ref[0, :, pl.ds(pl.multiple_of(source * WIDTH, WIDTH), WIDTH)] = block[...]
+        out_ref[0, :, pl.ds(pl.multiple_of(source * WIDTH, WIDTH), WIDTH)] = block[rows, :]
 
 
 def local(queries, suffix_keys, suffix_values, prefix_keys, prefix_values, hit_len, suffix_len, page_map):
@@ -182,8 +183,9 @@
     blocks = sum(sent, [])
     return pl.pallas_call(
         gather_kernel,
+        grid=(2,),
         in_specs=[SMEM] + [VMEM] * 8,
-        out_specs=VMEM,
+        out_specs=pl.BlockSpec((1, ROWS // 2, 8 * WIDTH), lambda i: (0, i, 0)),
         out_shape=jax.ShapeDtypeStruct((1, ROWS, 8 * WIDTH), BF16),
         compiler_params=PARAMS,
         name="gather_blocks",

time: 83.7 us -> 83.5 us (level)
  no operation moved by 1% of the time
where the time goes in v5:
time: 83.5 us
  blocking collectives  36.9 us (44%)
  Pallas kernels  27.8 us (33%)
  starting transfers between devices  15.5 us (19%)
  other arithmetic  1.68 us (2%)
  waiting for transfers between devices  1.44 us (2%)
    all_to_all x1, blocking collectives, local(): lax.all_to_all(packed, DEVICES, split_axis=0, concat_axis=0, tiled=True)  36.9 us
    pallas_call x3, Pallas kernels, local(): pl.pallas_call(functools.partial(later_kernel, shifts), in_specs=[SMEM] +...  18.8 us
    ppermute x7, starting transfers between devices, send(): lax.ppermute(x, 'tensor', [(z, (z + d) % 8) for z in range(8)])  15.5 us
    pallas_call x1, Pallas kernels, local(): pl.pallas_call(functools.partial(first_kernel, GROUPS[0]), in_specs=[SMEM...  7.46 us
    concatenate x1, other arithmetic, local(): packed = jnp.concatenate([prefix_keys[0], prefix_values[0]], axis=1)  1.68 us
  transfers between devices with their start and end apart: 7, of which 1 were waited for; matrix products, arithmetic and copies ran while one was open for 0% of the time, Pallas kernels for 22%

profile of v5, /device:TPU:1, one launch (start us, length us, event | category | flops | bytes accessed | tf_op | source)
XLA Modules:
  0.0 83.5 jit_solution(17171014819087750589)
XLA Ops:
  0.0 1.7 %pad_maximum_fusion = bf16[32,256,128]{2,1,0:T(8,128)(2,1)S(1)} fusion(bf16[32,128,128]{2,1,0:T(8,128)(2,1)} %bitcast.17, bf16[32,128,128]{2,1,0:T(8,128)(2,1)} %bitcast.18), kind=kLoop, calls=%fused_computation | loop fusion | flops 4194304 | bytes 4194304 | tf_op jit(solution)/shard_map/concatenate | solution.py:151
  1.7 0.0 copy-start
  1.7 0.0 copy-start.1
  1.7 0.0 copy-start.2
  1.7 0.0 copy-start.3
  1.7 0.0 copy-start.4
  1.7 0.0 copy-start.5
  1.8 36.9 %all_to_all.5.buf_ref = bf16[32,256,128]{2,1,0:T(8,128)(2,1)S(1)} all-to-all(bf16[32,256,128]{2,1,0:T(8,128)(2,1)S(1)} %pad_maximum_fusion), channel_id=1, replica_groups=mesh['dp'=4,'cache'=8,'tensor'=8] {'dp','cache'}, dimensions={0} | all-to-all | bytes 4194304 | tf_op jit(solution)/shard_map/all_to_all | solution.py:152
  38.7 0.0 copy-done
  38.7 0.0 copy-done.1
  38.7 0.0 copy-done.2
  38.7 0.0 copy-done.3
  38.7 0.0 copy-done.4
  38.7 0.0 copy-done.5
  38.7 7.5 %attend_first.1 = (s32[4]{0:T(128)S(1)}, bf16[4096,128]{1,0:T(8,128)(2,1)S(1)}, bf16[4096,256]{1,0:T(8,128)(2,1)S(1)}, bf16[32,2048]{1,0:T(8,128)(2,1)S(1)}, bf16[32,2048]{1,0:T(8,128)(2,1)S(1)}) custom-call(s32[32]{0:T(128)S(1)} %copy-done.4, s32[32]{0:T(128)S(1)} %copy-done.5, s32[32,32]{1,0:T(8,128)S(1)} %copy-done.3, bf16[8,32,2048]{2,1,0:T(8,128)(2,1)S(1)} %bitcast.5, ...), custom_call_target="tpu_custom_call" | custom-call | tf_op jit(solution)/shard_map/attend_first/pallas_call | solution.py:155
  46.2 4.4 %collective-permute-start = (bf16[32,2048]{1,0:T(8,128)(2,1)S(1)}, bf16[32,2048]{1,0:T(8,128)(2,1)S(1)}, u32[]{:S(2)}, u32[]{:S(2)}) collective-permute-start(bf16[32,2048]{1,0:T(8,128)(2,1)S(1)} %get-tuple-element.16), channel_id=1, source_target_pairs={{0,3},{1,4},{2,5},{3,6},{4,7},{5,0},{6,1},{7,2},{8,11},{9,12},{10,... | collective-permute-start | bytes 393224 | tf_op jit(solution)/shard_map/ppermute | solution.py:165
  50.6 2.4 %collective-permute-start.1 = (bf16[32,2048]{1,0:T(8,128)(2,1)S(1)}, bf16[32,2048]{1,0:T(8,128)(2,1)S(1)}, u32[]{:S(2)}, u32[]{:S(2)}) collective-permute-start(bf16[32,2048]{1,0:T(8,128)(2,1)S(1)} %get-tuple-element.17), channel_id=1, source_target_pairs={{0,5},{1,6},{2,7},{3,0},{4,1},{5,2},{6,3},{7,4},{8,13},{9,14},{10,... | collective-permute-start | bytes 393224 | tf_op jit(solution)/shard_map/ppermute | solution.py:165
  53.0 9.1 %attend_later.3 = (bf16[32,2048]{1,0:T(8,128)(2,1)S(1)}, bf16[32,2048]{1,0:T(8,128)(2,1)S(1)}, bf16[32,2048]{1,0:T(8,128)(2,1)S(1)}) custom-call(s32[4]{0:T(128)S(1)} %get-tuple-element.15.place, bf16[8,32,2048]{2,1,0:T(8,128)(2,1)S(1)} %bitcast.6, bf16[256,128]{1,0:T(8,128)(2,1)S(1)} %bitcast.10, bf16[256,128]{1,0:T(8,128)(2,1)S(1)} %bitcast.14, ...), custom_call_target="tpu_custom_call" | custom-call | tf_op jit(solution)/shard_map/attend_later/pallas_call | solution.py:174
  62.1 4.7 %collective-permute-start.2 = (bf16[32,2048]{1,0:T(8,128)(2,1)S(1)}, bf16[32,2048]{1,0:T(8,128)(2,1)S(1)}, u32[]{:S(2)}, u32[]{:S(2)}) collective-permute-start(bf16[32,2048]{1,0:T(8,128)(2,1)S(1)} %get-tuple-element.20), channel_id=1, source_target_pairs={{0,4},{1,5},{2,6},{3,7},{4,0},{5,1},{6,2},{7,3},{8,12},{9,13},{10,... | collective-permute-start | bytes 393224 | tf_op jit(solution)/shard_map/ppermute | solution.py:165
  66.8 0.0 collective-permute-start.3
  66.8 2.4 %collective-permute-start.4 = (bf16[32,2048]{1,0:T(8,128)(2,1)S(1)}, bf16[32,2048]{1,0:T(8,128)(2,1)S(1)}, u32[]{:S(2)}, u32[]{:S(2)}) collective-permute-start(bf16[32,2048]{1,0:T(8,128)(2,1)S(1)} %get-tuple-element.22), channel_id=1, source_target_pairs={{0,2},{1,3},{2,4},{3,5},{4,6},{5,7},{6,0},{7,1},{8,10},{9,11},{10,... | collective-permute-start | bytes 393224 | tf_op jit(solution)/shard_map/ppermute | solution.py:165
  69.2 0.0 collective-permute-done.refs_0_
  69.2 0.0 collective-permute-done.1.refs_1_
  69.2 6.3 %attend_later.4 = (bf16[32,2048]{1,0:T(8,128)(2,1)S(1)}, bf16[32,2048]{1,0:T(8,128)(2,1)S(1)}) custom-call(s32[4]{0:T(128)S(1)} %get-tuple-element.15.place, bf16[8,32,2048]{2,1,0:T(8,128)(2,1)S(1)} %bitcast.7, bf16[256,128]{1,0:T(8,128)(2,1)S(1)} %bitcast.11, bf16[256,128]{1,0:T(8,128)(2,1)S(1)} %bitcast.15, bf16[4096,128]{1,0:T(8,128)(2,1)S(1)} %get-tuple-element.18.k_ref, ...), custom_call_target="tpu_custom_call" | custom-call | tf_op jit(solution)/shard_map/attend_later/pallas_call | solution.py:174
  75.4 0.8 %collective-permute-start.5 = (bf16[32,2048]{1,0:T(8,128)(2,1)S(1)}, bf16[32,2048]{1,0:T(8,128)(2,1)S(1)}, u32[]{:S(2)}, u32[]{:S(2)}) collective-permute-start(bf16[32,2048]{1,0:T(8,128)(2,1)S(1)} %get-tuple-element.23), channel_id=1, source_target_pairs={{0,7},{1,0},{2,1},{3,2},{4,3},{5,4},{6,5},{7,6},{8,15},{9,8},{10,9... | collective-permute-start | bytes 393224 | tf_op jit(solution)/shard_map/ppermute | solution.py:165
  76.3 0.7 collective-permute-start.6
  77.0 0.0 collective-permute-done.2.refs_0_.refs_2_
  77.0 3.4 %attend_later.5.refs_7_ = bf16[32,2048]{1,0:T(8,128)(2,1)S(1)} custom-call(s32[4]{0:T(128)S(1)} %get-tuple-element.15.place, bf16[8,32,2048]{2,1,0:T(8,128)(2,1)S(1)} %bitcast.8, bf16[256,128]{1,0:T(8,128)(2,1)S(1)} %bitcast.12, bf16[256,128]{1,0:T(8,128)(2,1)S(1)} %bitcast.16, bf16[4096,128]{1,0:T(8,128)(2,1)S(1)} %get-tuple-element.18.k_ref, ...), custom_call_target="tpu_custom_call" | custom-call | tf_op jit(solution)/shard_map/attend_later/pallas_call | solution.py:174
  80.4 0.0 collective-permute-done.3.refs_3_
  80.4 0.0 collective-permute-done.4.refs_4_
  80.5 1.4 %collective-permute-done.5.refs_5_ = bf16[32,2048]{1,0:T(8,128)(2,1)S(1)} collective-permute-done((bf16[32,2048]{1,0:T(8,128)(2,1)S(1)}, bf16[32,2048]{1,0:T(8,128)(2,1)S(1)}, u32[]{:S(2)}, u32[]{:S(2)}) %collective-permute-start.5) | collective-permute-done | bytes 131104 | tf_op jit(solution)/shard_map/ppermute | solution.py:165
  81.9 0.0 collective-permute-done.6.refs_6_
  81.9 1.6 %gather_blocks.1 = bf16[1,32,16384]{2,1,0:T(8,128)(2,1)} custom-call(s32[4]{0:T(128)S(1)} %get-tuple-element.15.place, bf16[32,2048]{1,0:T(8,128)(2,1)S(1)} %collective-permute-done.refs_0_, bf16[32,2048]{1,0:T(8,128)(2,1)S(1)} %collective-permute-done.1.refs_1_, bf16[32,2048]{1,0:T(8,128)(2,1)S(1)} %collective-permute-done.2.refs_0_.refs_2_, ...), custom_call_target="tpu_custom_call" | custom-call | tf_op jit(solution)/shard_map/gather_blocks/pallas_call | solution.py:184
Async XLA Ops:
  1.7 37.0 %copy-start = (bf16[1,256,2048]{2,1,0:T(8,128)(2,1)S(1)}, bf16[1,256,2048]{2,1,0:T(8,128)(2,1)}, u32[]{:S(2)}) copy-start(bf16[1,256,2048]{2,1,0:T(8,128)(2,1)} %param.8) | copy-start | bytes 3145732
  1.7 37.0 %copy-start.1 = (bf16[1,256,128]{2,1,0:T(8,128)(2,1)S(1)}, bf16[1,256,128]{2,1,0:T(8,128)(2,1)}, u32[]{:S(2)}) copy-start(bf16[1,256,128]{2,1,0:T(8,128)(2,1)} %param.9) | copy-start | bytes 196612
  1.7 37.0 %copy-start.2 = (bf16[1,256,128]{2,1,0:T(8,128)(2,1)S(1)}, bf16[1,256,128]{2,1,0:T(8,128)(2,1)}, u32[]{:S(2)}) copy-start(bf16[1,256,128]{2,1,0:T(8,128)(2,1)} %param.10) | copy-start | bytes 196612
  1.7 37.0 %copy-start.3 = (s32[32,32]{1,0:T(8,128)S(1)}, s32[32,32]{1,0:T(8,128)}, u32[]{:S(2)}) copy-start(s32[32,32]{1,0:T(8,128)} %page_map.1) | copy-start | bytes 12292
  1.7 37.0 %copy-start.4 = (s32[32]{0:T(128)S(1)}, s32[32]{0:T(128)}, u32[]{:S(2)}) copy-start(s32[32]{0:T(128)} %hit_len.1) | copy-start | bytes 388
  1.7 37.0 %copy-start.5 = (s32[32]{0:T(128)S(1)}, s32[32]{0:T(128)}, u32[]{:S(2)}) copy-start(s32[32]{0:T(128)} %suffix_len.1) | copy-start | bytes 388
  46.2 23.0 %collective-permute-start = (bf16[32,2048]{1,0:T(8,128)(2,1)S(1)}, bf16[32,2048]{1,0:T(8,128)(2,1)S(1)}, u32[]{:S(2)}, u32[]{:S(2)}) collective-permute-start(bf16[32,2048]{1,0:T(8,128)(2,1)S(1)} %get-tuple-element.16), channel_id=1, source_target_pairs={{0,3},{1,4},{2,5},{3,6},{4,7},{5,0},{6,1},{7,2},{8,11},{9,12},{10,... | collective-permute-start | bytes 393224 | tf_op jit(solution)/shard_map/ppermute | solution.py:165
  50.6 18.6 %collective-permute-start.1 = (bf16[32,2048]{1,0:T(8,128)(2,1)S(1)}, bf16[32,2048]{1,0:T(8,128)(2,1)S(1)}, u32[]{:S(2)}, u32[]{:S(2)}) collective-permute-start(bf16[32,2048]{1,0:T(8,128)(2,1)S(1)} %get-tuple-element.17), channel_id=1, source_target_pairs={{0,5},{1,6},{2,7},{3,0},{4,1},{5,2},{6,3},{7,4},{8,13},{9,14},{10,... | collective-permute-start | bytes 393224 | tf_op jit(solution)/shard_map/ppermute | solution.py:165
  62.1 14.9 %collective-permute-start.2 = (bf16[32,2048]{1,0:T(8,128)(2,1)S(1)}, bf16[32,2048]{1,0:T(8,128)(2,1)S(1)}, u32[]{:S(2)}, u32[]{:S(2)}) collective-permute-start(bf16[32,2048]{1,0:T(8,128)(2,1)S(1)} %get-tuple-element.20), channel_id=1, source_target_pairs={{0,4},{1,5},{2,6},{3,7},{4,0},{5,1},{6,2},{7,3},{8,12},{9,13},{10,... | collective-permute-start | bytes 393224 | tf_op jit(solution)/shard_map/ppermute | solution.py:165
  66.8 13.6 %collective-permute-start.3 = (bf16[32,2048]{1,0:T(8,128)(2,1)S(1)}, bf16[32,2048]{1,0:T(8,128)(2,1)S(1)}, u32[]{:S(2)}, u32[]{:S(2)}) collective-permute-start(bf16[32,2048]{1,0:T(8,128)(2,1)S(1)} %get-tuple-element.21), channel_id=1, source_target_pairs={{0,6},{1,7},{2,0},{3,1},{4,2},{5,3},{6,4},{7,5},{8,14},{9,15},{10,... | collective-permute-start | bytes 393224 | tf_op jit(solution)/shard_map/ppermute | solution.py:165
  66.8 13.6 %collective-permute-start.4 = (bf16[32,2048]{1,0:T(8,128)(2,1)S(1)}, bf16[32,2048]{1,0:T(8,128)(2,1)S(1)}, u32[]{:S(2)}, u32[]{:S(2)}) collective-permute-start(bf16[32,2048]{1,0:T(8,128)(2,1)S(1)} %get-tuple-element.22), channel_id=1, source_target_pairs={{0,2},{1,3},{2,4},{3,5},{4,6},{5,7},{6,0},{7,1},{8,10},{9,11},{10,... | collective-permute-start | bytes 393224 | tf_op jit(solution)/shard_map/ppermute | solution.py:165
  75.4 6.4 %collective-permute-start.5 = (bf16[32,2048]{1,0:T(8,128)(2,1)S(1)}, bf16[32,2048]{1,0:T(8,128)(2,1)S(1)}, u32[]{:S(2)}, u32[]{:S(2)}) collective-permute-start(bf16[32,2048]{1,0:T(8,128)(2,1)S(1)} %get-tuple-element.23), channel_id=1, source_target_pairs={{0,7},{1,0},{2,1},{3,2},{4,3},{5,4},{6,5},{7,6},{8,15},{9,8},{10,9... | collective-permute-start | bytes 393224 | tf_op jit(solution)/shard_map/ppermute | solution.py:165
  76.3 5.6 %collective-permute-start.6 = (bf16[32,2048]{1,0:T(8,128)(2,1)S(1)}, bf16[32,2048]{1,0:T(8,128)(2,1)S(1)}, u32[]{:S(2)}, u32[]{:S(2)}) collective-permute-start(bf16[32,2048]{1,0:T(8,128)(2,1)S(1)} %get-tuple-element.24), channel_id=1, source_target_pairs={{0,1},{1,2},{2,3},{3,4},{4,5},{5,6},{6,7},{7,0},{8,9},{9,10},{10,1... | collective-permute-start | bytes 393224 | tf_op jit(solution)/shard_map/ppermute | solution.py:165
